TPU v7x, 32 devices: a whole 2x2x4 slice. The times are simulated.
32 devices in a mesh: ctx: 16 (over z, x, core), head: 2 (over y).
Axes of the slice: x: 2, y: 2, z: 4, core: 2. Of those that a mesh axis runs over, the one named last changes fastest.
Arguments:
- q_nope: bfloat16 [4096, 16, 128], P('ctx', 'head'), may hold values from -6 to 6
- q_rope: bfloat16 [4096, 16, 64], P('ctx', 'head'), may hold values from -300 to 300
- c_kv: bfloat16 [4096, 512], P('ctx'), may hold values from -6 to 6
- k_rope: bfloat16 [4096, 64], P('ctx'), may hold values from -6 to 6
- block_pos: int32 [32], replicated, may hold values from 0 to 31, as said below
- w_uk: bfloat16 [16, 128, 512], P('head'), may hold values from -0.5 to 0.5
- w_uv: bfloat16 [16, 512, 128], P('head'), may hold values from -6 to 6
Outputs:
- attn_out: bfloat16 [4096, 16, 128], P('ctx', 'head')
Inputs may be any that keep to these rules, and one draw needn't show every extreme that they name: block_pos is the mirrored-pair order turned by some c: block_pos[2 s] = (s + c) mod 16 and block_pos[2 s + 1] = 31 - block_pos[2 s].
All inputs are finite; a program needn't handle non-finite values.
Results may differ from a plain program's by a relative error of at most 0.0072.
Values may be sent and summed in bfloat16 or wider, within the bound.
A program may use at most 64 MiB of HBM per device.

v0:
```python
import math

import jax
import jax.numpy as jnp
from jax import lax
from jax.sharding import PartitionSpec as P


def from_behind(array, axis, by):
    length = lax.axis_size(axis)
    return lax.ppermute(array, axis, [(i, (i + by) % length) for i in range(length)])


def per_device(q_nope, q_rope, c_kv, k_rope, block_pos, w_uk, w_uv):
    rows = q_nope.shape[0]
    blk = rows // 2
    lat_width = c_kv.shape[1]
    scale = 1.0 / math.sqrt(q_nope.shape[2] + q_rope.shape[2])
    cycle = lax.axis_size("ctx")
    place = lax.axis_index("ctx")
    span = jnp.arange(blk, dtype=jnp.int32)

    def positions(source):
        pair = lax.dynamic_slice_in_dim(block_pos, 2 * source, 2)
        return (pair[:, None] * blk + span[None, :]).reshape(-1)

    packed = jnp.concatenate([c_kv, k_rope], axis=1).reshape(blk, -1)
    from_lower = from_behind(packed, "ctx", 1)
    from_upper = from_behind(packed, "ctx", -1)
    far_lower = from_behind(from_lower, "ctx", 1)
    far_upper = from_behind(from_upper, "ctx", -1)
    pieces = [packed, from_lower, from_upper, far_lower, far_upper]
    keys = jnp.concatenate([piece.reshape(rows, -1) for piece in pieces], axis=0)
    kpos = jnp.concatenate(
        [positions((place - offset) % cycle) for offset in (0, 1, -1, 2, -2)], axis=0
    )
    qpos = positions(place)
    latent = keys[:, :lat_width]
    rotary = keys[:, lat_width:]
    q_lat = jnp.einsum("thn,hnl->thl", q_nope, w_uk, preferred_element_type=jnp.float32).astype(
        jnp.bfloat16
    )
    score = jnp.einsum("thl,kl->thk", q_lat, latent, preferred_element_type=jnp.float32)
    score = (
        score + jnp.einsum("thr,kr->thk", q_rope, rotary, preferred_element_type=jnp.float32)
    ) * scale
    visible = kpos[None, None, :] <= qpos[:, None, None]
    score = jnp.where(visible, score, -1e30)
    top = jnp.max(score, axis=2, keepdims=True)
    expo = jnp.where(visible, jnp.exp(score - top), 0.0)
    total = jnp.sum(expo, axis=2)
    weights = expo.astype(jnp.bfloat16)
    o_lat = jnp.einsum("thk,kl->thl", weights, latent, preferred_element_type=jnp.float32)
    o_lat = (o_lat / total[:, :, None]).astype(jnp.bfloat16)
    return jnp.einsum("thl,hlv->thv", o_lat, w_uv, preferred_element_type=jnp.float32).astype(
        jnp.bfloat16
    )


def solution(mesh):
    placed = (
        P("ctx", "head", None),
        P("ctx", "head", None),
        P("ctx", None),
        P("ctx", None),
        P(),
        P("head", None, None),
        P("head", None, None),
    )
    return jax.shard_map(
        per_device, mesh=mesh, in_specs=placed, out_specs=P("ctx", "head", None), check_vma=False
    )
```

profile of v0, /device:TPU:0, one launch (start us, length us, event | category | flops | bytes accessed | tf_op | source)
XLA Modules:
  0.0 53.7 jit_solution(14400083194421477711)
XLA Ops:
  0.0 0.0 copy-start
  0.0 1.0 %copy.12 = bf16[256,64]{1,0:T(8,128)(2,1)S(1)} copy(bf16[256,64]{0,1:T(8,128)(2,1)} %param.10) | data formatting | bytes 65536 | tf_op args[3]
  1.0 1.7 %pad_maximum_fusion = (bf16[256,576]{1,0:T(8,128)(2,1)S(1)}, bf16[1280,576]{1,0:T(8,128)(2,1)}) fusion(bf16[256,64]{1,0:T(8,128)(2,1)S(1)} %copy.12, bf16[256,512]{1,0:T(8,128)(2,1)} %param.9), kind=kLoop, calls=%fused_computation.19 | loop fusion | flops 589823 | bytes 917504 | tf_op jit(solution)/shard_map/concatenate | solution.py:27
  2.7 0.2 reshape.92
  3.0 5.5 %collective-permute-start.1 = (bf16[128,1152]{1,0:T(8,128)(2,1)S(1)}, bf16[128,1152]{1,0:T(8,128)(2,1)S(1)}, u32[]{:S(2)}, u32[]{:S(2)}) collective-permute-start(bf16[128,1152]{1,0:T(8,128)(2,1)S(1)} %reshape.92), channel_id=1, source_target_pairs={{0,30},{2,0},{4,2},{6,4},{8,6},{10,8},{12,10},{14,12},{16,14},{18,... | collective-permute-start | bytes 884744 | tf_op jit(solution)/shard_map/ppermute | solution.py:11
  8.4 0.0 collective-permute-start
  8.4 1.0 %dynamic-slice_multiply_fusion = (s32[2]{0:T(128)S(1)}, s32[2]{0:T(128)S(1)}, s32[2]{0:T(128)S(1)}, s32[2]{0:T(128)S(1)}, s32[2]{0:T(128)S(1)}, /*index=5*/s32[2]{0:T(128)S(1)}) fusion(s32[32]{0:T(128)} %param.11, s32[]{:T(128)S(6)} %select_n.58, s32[]{:T(128)S(6)} %select_n.55, s32[]{:T(128)S(6)} %select_n.53, s32[]{:T(128)S(6)} %select_n.51, ...), kind=kLoop, calls=%fused_computation.31 | loop fusion | flops 12 | bytes 120 | tf_op jit(solution)/shard_map/mul | solution.py:25
  9.4 0.1 add_bitcast_fusion
  9.5 0.1 constant_dynamic-update-slice_fusion
  9.5 0.1 constant_dynamic-update-slice_fusion.9
  9.6 0.1 constant_dynamic-update-slice_fusion.8
  9.7 0.1 constant_dynamic-update-slice_fusion.7
  9.8 0.1 constant_dynamic-update-slice_fusion.6
  9.8 7.5 %collective-permute-done = bf16[128,1152]{1,0:T(8,128)(2,1)S(1)} collective-permute-done((bf16[128,1152]{1,0:T(8,128)(2,1)S(1)}, bf16[128,1152]{1,0:T(8,128)(2,1)S(1)}, u32[]{:S(2)}, u32[]{:S(2)}) %collective-permute-start) | collective-permute-done | bytes 294944 | tf_op jit(solution)/shard_map/ppermute | solution.py:11
  17.3 0.0 collective-permute-start.2
  17.3 0.2 broadcast_compare_fusion
  17.5 0.2 reshape.93
  17.8 0.0 collective-permute-done.1
  17.8 4.5 %collective-permute-start.3 = (bf16[128,1152]{1,0:T(8,128)(2,1)S(1)}, bf16[128,1152]{1,0:T(8,128)(2,1)S(1)}, u32[]{:S(2)}, u32[]{:S(2)}) collective-permute-start(bf16[128,1152]{1,0:T(8,128)(2,1)S(1)} %collective-permute-done.1), channel_id=1, source_target_pairs={{0,30},{2,0},{4,2},{6,4},{8,6},{10,8},{12,10},{14,12},{16,14},{18,... | collective-permute-start | bytes 884744 | tf_op jit(solution)/shard_map/ppermute | solution.py:11
  22.3 0.0 copy-start.1
  22.3 0.8 %constant_dynamic-update-slice_fusion.4 = bf16[1280,576]{1,0:T(8,128)(2,1)} fusion(bf16[1280,576]{1,0:T(8,128)(2,1)} %get-tuple-element.6, bf16[256,576]{1,0:T(8,128)(2,1)S(1)} %reshape.93), kind=kLoop, calls=%fused_computation.24 | loop fusion | bytes 622592
  23.0 0.2 reshape.94
  23.2 0.8 %constant_dynamic-update-slice_fusion.3 = bf16[1280,576]{1,0:T(8,128)(2,1)} fusion(bf16[1280,576]{1,0:T(8,128)(2,1)} %constant_dynamic-update-slice_fusion.4, bf16[256,576]{1,0:T(8,128)(2,1)S(1)} %reshape.94), kind=kLoop, calls=%fused_computation.23 | loop fusion | bytes 622592
  24.0 2.1 %collective-permute-done.2 = bf16[128,1152]{1,0:T(8,128)(2,1)S(1)} collective-permute-done((bf16[128,1152]{1,0:T(8,128)(2,1)S(1)}, bf16[128,1152]{1,0:T(8,128)(2,1)S(1)}, u32[]{:S(2)}, u32[]{:S(2)}) %collective-permute-start.2) | collective-permute-done | bytes 294944 | tf_op jit(solution)/shard_map/ppermute | solution.py:11
  26.1 0.2 reshape.95
  26.3 0.8 %constant_dynamic-update-slice_fusion.2 = bf16[1280,576]{1,0:T(8,128)(2,1)} fusion(bf16[1280,576]{1,0:T(8,128)(2,1)} %constant_dynamic-update-slice_fusion.3, bf16[256,576]{1,0:T(8,128)(2,1)S(1)} %reshape.95), kind=kLoop, calls=%fused_computation.22 | loop fusion | bytes 622592
  27.1 0.0 collective-permute-done.3
  27.1 0.2 reshape.96
  27.3 0.8 %constant_dynamic-update-slice_fusion.1 = bf16[1280,576]{1,0:T(8,128)(2,1)} fusion(bf16[1280,576]{1,0:T(8,128)(2,1)} %constant_dynamic-update-slice_fusion.2, bf16[256,576]{1,0:T(8,128)(2,1)S(1)} %reshape.96), kind=kLoop, calls=%fused_computation.21 | loop fusion | bytes 622592 | tf_op jit(solution)/shard_map/concatenate | solution.py:33
  28.1 0.0 copy-done.1
  28.1 0.0 copy-start.3
  28.1 6.6 %fusion.22 = f32[1280,256,8]{0,1,2:T(8,128)} fusion(bf16[256,8,64]{0,2,1:T(8,128)(2,1)S(1)} %copy-done.1, bf16[1280,576]{1,0:T(8,128)(2,1)} %constant_dynamic-update-slice_fusion.1), kind=kOutput, calls=%fused_computation.18 | convolution fusion | flops 335544320 | bytes 11075584 | tf_op jit(solution)/shard_map/thr,kr->thk/dot_general | solution.py:45
  34.7 0.0 copy-done
  34.7 0.0 copy-done.3
  34.7 0.0 copy-start.2
  34.7 11.5 %fusion.23 = (f32[256,8]{0,1:T(8,128)S(1)}, bf16[256,8,1280]{2,0,1:T(8,128)(2,1)}) fusion(pred[256,1280]{1,0:T(8,128)(4,1)S(1)} %broadcast_compare_fusion, f32[1280,256,8]{0,1,2:T(8,128)} %fusion.22, bf16[8,128,512]{2,1,0:T(8,128)(2,1)S(1)} %copy-done, bf16[1280,576]{1,0:T(8,128)(2,1)} %constant_dynamic-update-slice_fusion.1, ...), kind=kOutput, calls=%fused_computation.37 | convolution fusion | flops 2972189952 | bytes 19275776 | tf_op jit(solution)/shard_map/sub | solution.py:50
  46.2 0.0 copy-done.2
  46.2 6.3 %fusion.17 = bf16[256,8,128]{2,0,1:T(8,128)(2,1)S(1)} fusion(bf16[8,512,128]{2,1,0:T(8,128)(2,1)S(1)} %copy-done.2, bf16[256,8,1280]{2,0,1:T(8,128)(2,1)} %get-tuple-element.14, f32[256,8]{0,1:T(8,128)S(1)} %get-tuple-element.13, bf16[1280,576]{1,0:T(8,128)(2,1)} %constant_dynamic-update-slice_fusion.1), kind=kOutput, calls=%fused_computation.14 | convolution fusion | flops 2955149312 | bytes 8134656 | tf_op jit(solution)/shard_map/thl,hlv->thv/dot_general | solution.py:55
  52.5 1.1 %copy.15 = bf16[256,8,128]{2,1,0:T(8,128)(2,1)} copy(bf16[256,8,128]{2,0,1:T(8,128)(2,1)S(1)} %fusion.17) | data formatting | bytes 1048576 | tf_op jit(solution)/shard_map/convert_element_type | solution.py:55
  (1 shorter events, 0.0 us)
Async XLA Ops:
  0.0 34.7 %copy-start = (bf16[8,128,512]{2,1,0:T(8,128)(2,1)S(1)}, bf16[8,128,512]{2,1,0:T(8,128)(2,1)}, u32[]{:S(2)}) copy-start(bf16[8,128,512]{2,1,0:T(8,128)(2,1)} %param.12) | copy-start | bytes 3145732
  3.0 14.8 %collective-permute-start.1 = (bf16[128,1152]{1,0:T(8,128)(2,1)S(1)}, bf16[128,1152]{1,0:T(8,128)(2,1)S(1)}, u32[]{:S(2)}, u32[]{:S(2)}) collective-permute-start(bf16[128,1152]{1,0:T(8,128)(2,1)S(1)} %reshape.92), channel_id=1, source_target_pairs={{0,30},{2,0},{4,2},{6,4},{8,6},{10,8},{12,10},{14,12},{16,14},{18,... | collective-permute-start | bytes 884744 | tf_op jit(solution)/shard_map/ppermute | solution.py:11
  8.4 8.8 %collective-permute-start = (bf16[128,1152]{1,0:T(8,128)(2,1)S(1)}, bf16[128,1152]{1,0:T(8,128)(2,1)S(1)}, u32[]{:S(2)}, u32[]{:S(2)}) collective-permute-start(bf16[128,1152]{1,0:T(8,128)(2,1)S(1)} %reshape.92), channel_id=1, source_target_pairs={{0,2},{2,4},{4,6},{6,8},{8,10},{10,12},{12,14},{14,16},{16,18},{18... | collective-permute-start | bytes 884744 | tf_op jit(solution)/shard_map/ppermute | solution.py:11
  17.3 8.8 %collective-permute-start.2 = (bf16[128,1152]{1,0:T(8,128)(2,1)S(1)}, bf16[128,1152]{1,0:T(8,128)(2,1)S(1)}, u32[]{:S(2)}, u32[]{:S(2)}) collective-permute-start(bf16[128,1152]{1,0:T(8,128)(2,1)S(1)} %collective-permute-done), channel_id=1, source_target_pairs={{0,2},{2,4},{4,6},{6,8},{8,10},{10,12},{12,14},{14,16},{16,18},{18... | collective-permute-start | bytes 884744 | tf_op jit(solution)/shard_map/ppermute | solution.py:11
  17.8 9.3 %collective-permute-start.3 = (bf16[128,1152]{1,0:T(8,128)(2,1)S(1)}, bf16[128,1152]{1,0:T(8,128)(2,1)S(1)}, u32[]{:S(2)}, u32[]{:S(2)}) collective-permute-start(bf16[128,1152]{1,0:T(8,128)(2,1)S(1)} %collective-permute-done.1), channel_id=1, source_target_pairs={{0,30},{2,0},{4,2},{6,4},{8,6},{10,8},{12,10},{14,12},{16,14},{18,... | collective-permute-start | bytes 884744 | tf_op jit(solution)/shard_map/ppermute | solution.py:11
  22.3 5.8 %copy-start.1 = (bf16[256,8,64]{0,2,1:T(8,128)(2,1)S(1)}, bf16[256,8,64]{0,2,1:T(8,128)(2,1)}, u32[]{:S(2)}) copy-start(bf16[256,8,64]{0,2,1:T(8,128)(2,1)} %param.8) | copy-start | bytes 786436
  28.1 6.6 %copy-start.3 = (bf16[256,8,128]{2,1,0:T(8,128)(2,1)S(1)}, bf16[256,8,128]{2,1,0:T(8,128)(2,1)}, u32[]{:S(2)}) copy-start(bf16[256,8,128]{2,1,0:T(8,128)(2,1)} %param.7) | copy-start | bytes 1572868
  34.7 11.5 %copy-start.2 = (bf16[8,512,128]{2,1,0:T(8,128)(2,1)S(1)}, bf16[8,512,128]{2,1,0:T(8,128)(2,1)}, u32[]{:S(2)}) copy-start(bf16[8,512,128]{2,1,0:T(8,128)(2,1)} %param.13) | copy-start | bytes 3145732
where the time goes:
time: 53.9 us; the launch traced here: 53.7 us
  matrix products  24.4 us (45%)
  starting transfers between devices  9.97 us (18%)
  waiting for transfers between devices  9.57 us (18%)
  local copies, waits for them, and re-layouts  6.25 us (12%)
  other arithmetic  3.38 us (6%)
    sub x1, matrix products, per_device(): expo = jnp.where(visible, jnp.exp(score - top), 0.0)  11.5 us
    ppermute x4, starting transfers between devices, from_behind(): lax.ppermute(array, axis, [(i, (i + by) % length) for i in range(length)])  9.97 us
    ppermute x4, waiting for transfers between devices, from_behind(): lax.ppermute(array, axis, [(i, (i + by) % length) for i in range(length)])  9.57 us
    dot_general x1, matrix products, per_device(): jnp.einsum('thr,kr->thk', q_rope, rotary, preferred_element_type=jnp.floa...  6.58 us
    dot_general x1, matrix products, per_device(): jnp.einsum('thl,hlv->thv', o_lat, w_uv, preferred_element_type=jnp.float32)  6.33 us
    unnamed x12, local copies, waits for them, and re-layouts  3.27 us
    concatenate x1, other arithmetic, per_device(): packed = jnp.concatenate([c_kv, k_rope], axis=1).reshape(blk, -1)  1.75 us
    convert_element_type x1, local copies, waits for them, and re-layouts, per_device(): jnp.einsum('thl,hlv->thv', o_lat, w_uv, preferred_element_type=jnp.float32)  1.14 us
  transfers between devices with their start and end apart: 4, of which 2 were waited for; matrix products, arithmetic and copies ran while one was open for 8% of the time, Pallas kernels for 0%

commit v1 on v0

v1 whole, which is shorter than its diff:
```python
import functools
import math

import jax
import jax.numpy as jnp
from jax import lax
from jax.experimental import pallas as pl
from jax.experimental.pallas import tpu as pltpu
from jax.sharding import PartitionSpec as P

MESH = pl.DeviceIdType.MESH
LANES = 128
PIECES = ((0, 5), (5, 4))
PARTNER, NEAR, FAR, WIDE = 0, 1, 2, 3


def nt_dot(a, b):
    return lax.dot_general(a, b, (((1,), (1,)), ((), ())), preferred_element_type=jnp.float32)


def attention_kernel(
    factor,
    pos_ref, ckv_ref, krope_ref, qn_hbm, qr_hbm, wuk_hbm, wuv_hbm, out_ref,
    qn, qr, wuk, wuv, flat, flat_rope, qs, held, keys, acc, top_s, sum_s,
    load_sem, send_sem, recv_sem,
):
    n = lax.axis_size("ctx")
    me = lax.axis_index("ctx")
    heads = qn.shape[1]
    blk = ckv_ref.shape[0] // 2
    lat = ckv_ref.shape[1]
    rope = krope_ref.shape[1]
    odd = lax.rem(me, 2)

    def at(by):
        return lax.rem(me + by + n, n)

    partner = at(1 - 2 * odd)
    near = at(2 * odd - 1)
    far = at(4 * odd - 2)
    wide = at(2 - 4 * odd)

    loads = [
        pltpu.make_async_copy(a, b, load_sem.at[i])
        for i, (a, b) in enumerate(
            ((qn_hbm, qn), (wuk_hbm, wuk), (qr_hbm, qr), (wuv_hbm, wuv))
        )
    ]
    for load in loads:
        load.start()

    barrier = pltpu.get_barrier_semaphore()
    for other in (partner, near, far, wide):
        pl.semaphore_signal(barrier, inc=1, device_id={"ctx": other}, device_id_type=MESH)

    for c in range(4):
        held[4, c] = ckv_ref[:blk, c * LANES:(c + 1) * LANES]
        held[4, 5 + c] = ckv_ref[blk:, c * LANES:(c + 1) * LANES]
    held[4, 4, :, :rope] = krope_ref[:blk, :]
    held[4, 4, :, rope:] = krope_ref[blk:, :]
    pl.semaphore_wait(barrier, 4)

    def send(slot_from, slot_to, piece, target):
        start, size = PIECES[piece]
        return pltpu.make_async_remote_copy(
            src_ref=held.at[slot_from, pl.ds(start, size)],
            dst_ref=held.at[slot_to, pl.ds(start, size)],
            send_sem=send_sem.at[slot_to, piece],
            recv_sem=recv_sem.at[slot_to, piece],
            device_id={"ctx": target},
            device_id_type=MESH,
        )

    copies = {}
    for piece in (0, 1):
        for slot, target in ((NEAR, near), (FAR, wide), (PARTNER, partner)):
            copies[slot, piece] = send(4, slot, piece, target)
            copies[slot, piece].start()
        copies[WIDE, piece] = send(NEAR, WIDE, piece, partner)

    loads[0].wait()
    flat[...] = qn[...].astype(jnp.float32).reshape(flat.shape)
    loads[1].wait()
    loads[2].wait()
    flat_rope[...] = qr[...].astype(jnp.float32).reshape(flat_rope.shape)

    for h in range(heads):
        for b in range(2):
            rows = pl.ds(b * blk * heads + h, blk, stride=heads)
            part = flat[rows, :].astype(jnp.bfloat16)
            into = pl.ds(h * blk, blk)
            qs[b, into, :lat] = jnp.dot(
                part, wuk[h], preferred_element_type=jnp.float32
            ).astype(jnp.bfloat16)
            turned = flat_rope[rows, :].astype(jnp.bfloat16)
            qs[b, into, lat:lat + rope] = turned
            qs[b, into, lat + rope:] = turned

    my_pos = pos_ref[2 * me]
    lane = lax.broadcasted_iota(jnp.int32, (blk, LANES), 1)
    chunk = qs.shape[1] // 2

    def gather(slot, low_at, high_at):
        for base, first in ((low_at, 0), (high_at, 5)):
            for c in range(4):
                keys[pl.ds(base, blk), c * LANES:(c + 1) * LANES] = held[slot, first + c]
        both = held[slot, 4]
        zero = jnp.zeros_like(both)
        keys[pl.ds(low_at, blk), lat:] = jnp.where(lane < rope, both, zero)
        keys[pl.ds(high_at, blk), lat:] = jnp.where(lane < rope, zero, both)

    def fold(b, rows, width, hide, first):
        score = nt_dot(qs[b, rows, :], keys[:width, :]) * factor
        score = hide(score)
        best = jnp.max(score, axis=1, keepdims=True)
        if not first:
            old = top_s[b, rows, :1]
            best = jnp.maximum(best, old)
        expo = jnp.exp2(score - best)
        total = jnp.sum(expo, axis=1, keepdims=True)
        part = jnp.dot(
            expo.astype(jnp.bfloat16), keys[:width, :lat], preferred_element_type=jnp.float32
        )
        if not first:
            shrink = jnp.exp2(old - best)
            total = total + sum_s[b, rows, :1] * shrink
            part = part + acc[b, rows, :] * shrink
        acc[b, rows, :] = part
        top_s[b, rows, :] = jnp.broadcast_to(best, (chunk, LANES))
        sum_s[b, rows, :] = jnp.broadcast_to(total, (chunk, LANES))

    def stage(slots, sources, first):
        count = len(slots)
        for i, slot in enumerate(slots):
            gather(slot, i * blk, (count + i) * blk)
        at_key = lax.broadcasted_iota(jnp.int32, (1, count * blk), 1) // blk
        low_bias = jnp.zeros((1, count * blk), jnp.float32)
        high_bias = jnp.zeros((1, count * blk), jnp.float32)
        for i, source in enumerate(sources):
            if source is None:
                continue
            theirs = pos_ref[2 * source]
            low = jnp.where(theirs <= my_pos, 0.0, -1e30)
            high = jnp.where(theirs >= my_pos, 0.0, -1e30)
            low_bias = jnp.where(at_key == i, low, low_bias)
            high_bias = jnp.where(at_key == i, high, high_bias)

        def hide_low(score):
            if not first:
                return score + low_bias
            token = lax.rem(lax.broadcasted_iota(jnp.int32, score.shape, 0), blk)
            key = lax.broadcasted_iota(jnp.int32, score.shape, 1)
            return jnp.where((key <= token) | (key >= blk), score + low_bias, -1e30)

        def hide_high(score):
            half = count * blk
            if not first:
                return jnp.concatenate([score[:, :half], score[:, half:] + high_bias], axis=1)
            token = lax.rem(lax.broadcasted_iota(jnp.int32, (score.shape[0], half), 0), blk)
            key = lax.broadcasted_iota(jnp.int32, (score.shape[0], half), 1)
            right = jnp.where(
                (key <= token) | (key >= blk), score[:, half:] + high_bias, -1e30
            )
            return jnp.concatenate([score[:, :half], right], axis=1)

        def body(c, carry):
            rows = pl.ds(pl.multiple_of(c * chunk, chunk), chunk)
            fold(1, rows, 2 * count * blk, hide_high, first)
            fold(0, rows, count * blk, hide_low, first)
            return carry

        lax.fori_loop(0, 2, body, 0)

    copies[PARTNER, 0].wait_recv()
    copies[PARTNER, 1].wait_recv()
    stage((4, PARTNER), (None, partner), True)

    for piece in (0, 1):
        copies[NEAR, piece].wait_recv()
        copies[WIDE, piece].start()
    copies[FAR, 0].wait_recv()
    copies[FAR, 1].wait_recv()
    stage((NEAR, FAR), (near, far), False)
    copies[WIDE, 0].wait_recv()
    copies[WIDE, 1].wait_recv()
    stage((WIDE,), (wide,), False)

    loads[3].wait()
    for h in range(heads):
        for b in range(2):
            rows = pl.ds(h * blk, blk)
            o_lat = (acc[b, rows, :] / sum_s[b, rows, :1]).astype(jnp.bfloat16)
            flat[pl.ds(b * blk * heads + h, blk, stride=heads), :] = jnp.dot(
                o_lat, wuv[h], preferred_element_type=jnp.float32
            )
    out_ref[...] = flat[...].reshape(out_ref.shape).astype(jnp.bfloat16)
    for key in copies:
        copies[key].wait_send()


def per_device(q_nope, q_rope, c_kv, k_rope, block_pos, w_uk, w_uv):
    rows, heads, nope = q_nope.shape
    blk = rows // 2
    lat = c_kv.shape[1]
    rope = k_rope.shape[1]
    factor = math.log2(math.e) / math.sqrt(nope + rope)
    vmem = pl.BlockSpec(memory_space=pltpu.VMEM)
    anywhere = pl.BlockSpec(memory_space=pl.ANY)
    bf16, f32 = jnp.bfloat16, jnp.float32
    return pl.pallas_call(
        functools.partial(attention_kernel, factor),
        out_shape=jax.ShapeDtypeStruct((rows, heads, w_uv.shape[2]), bf16),
        in_specs=[pl.BlockSpec(memory_space=pltpu.SMEM), vmem, vmem] + [anywhere] * 4,
        out_specs=vmem,
        scratch_shapes=[
            pltpu.VMEM(q_nope.shape, bf16),
            pltpu.VMEM(q_rope.shape, bf16),
            pltpu.VMEM(w_uk.shape, bf16),
            pltpu.VMEM(w_uv.shape, bf16),
            pltpu.VMEM((rows * heads, nope), f32),
            pltpu.VMEM((rows * heads, rope), f32),
            pltpu.VMEM((2, blk * heads, lat + 2 * rope), bf16),
            pltpu.VMEM((5, 9, blk, LANES), bf16),
            pltpu.VMEM((4 * blk, lat + 2 * rope), bf16),
            pltpu.VMEM((2, blk * heads, lat), f32),
            pltpu.VMEM((2, blk * heads, LANES), f32),
            pltpu.VMEM((2, blk * heads, LANES), f32),
            pltpu.SemaphoreType.DMA((4,)),
            pltpu.SemaphoreType.DMA((4, 2)),
            pltpu.SemaphoreType.DMA((4, 2)),
        ],
        compiler_params=pltpu.CompilerParams(
            collective_id=0, has_side_effects=True, vmem_limit_bytes=48 * 1024 * 1024
        ),
        cost_estimate=pl.CostEstimate(
            flops=6 * 10**9, bytes_accessed=5 * 10**6, transcendentals=2 * 10**6
        ),
    )(block_pos, c_kv, k_rope, q_nope, q_rope, w_uk, w_uv)


def solution(mesh):
    placed = (
        P("ctx", "head", None),
        P("ctx", "head", None),
        P("ctx", None),
        P("ctx", None),
        P(),
        P("head", None, None),
        P("head", None, None),
    )
    return jax.shard_map(
        per_device, mesh=mesh, in_specs=placed, out_specs=P("ctx", "head", None), check_vma=False
    )
```

time: 53.9 us -> 39.5 us (0.73)
  the two profiles are of different devices: /device:TPU:0 before, /device:TPU:1 now
where the time goes in v1:
time: 39.5 us; the launch traced here: 39.3 us
  Pallas kernels  33.7 us (85%)
  local copies, waits for them, and re-layouts  5.49 us (14%)
    pallas_call x1, Pallas kernels, per_device(): pl.pallas_call(functools.partial(attention_kernel, factor), out_shape=jax...  33.7 us
    unnamed x13, local copies, waits for them, and re-layouts  5.49 us

profile of v1, /device:TPU:1, one launch (start us, length us, event | category | flops | bytes accessed | tf_op | source)
XLA Modules:
  0.0 39.3 jit_solution(5933976283161003356)
XLA Ops:
  0.0 0.0 copy-start.2
  0.0 0.9 %copy.8.krope_ref = bf16[256,64]{1,0:T(8,128)(2,1)S(1)} copy(bf16[256,64]{0,1:T(8,128)(2,1)} %param.10) | data formatting | bytes 65536 | tf_op args[3]
  0.9 0.0 copy-start.3
  0.9 0.0 copy-start.4
  1.0 1.3 %copy.9.qr_hbm = bf16[256,8,64]{2,1,0:T(8,128)(2,1)S(1)} copy(bf16[256,8,64]{0,2,1:T(8,128)(2,1)} %param.8) | data formatting | bytes 524288 | tf_op args[1]
  2.3 0.0 copy-done.2
  2.3 0.0 copy-done.3
  2.3 0.0 copy-done.4
  2.3 0.0 copy-start
  2.3 1.2 %copy-done = bf16[8,128,512]{2,1,0:T(8,128)(2,1)S(1)} copy-done((bf16[8,128,512]{2,1,0:T(8,128)(2,1)S(1)}, bf16[8,128,512]{2,1,0:T(8,128)(2,1)}, u32[]{:S(2)}) %copy-start) | copy-done | bytes 1048600
  3.5 0.0 copy-start.1
  3.5 1.2 %copy-done.1 = bf16[8,512,128]{2,1,0:T(8,128)(2,1)S(1)} copy-done((bf16[8,512,128]{2,1,0:T(8,128)(2,1)S(1)}, bf16[8,512,128]{2,1,0:T(8,128)(2,1)}, u32[]{:S(2)}) %copy-start.1) | copy-done | bytes 1048600
  4.8 33.7 %shard_map.73 = bf16[256,8,128]{2,1,0:T(8,128)(2,1)S(1)} custom-call(s32[32]{0:T(128)S(1)} %copy-done.4, bf16[256,512]{1,0:T(8,128)(2,1)S(1)} %copy-done.3, bf16[256,64]{1,0:T(8,128)(2,1)S(1)} %copy.8.krope_ref, bf16[256,8,128]{2,1,0:T(8,128)(2,1)S(1)} %copy-done.2, bf16[256,8,64]{2,1,0:T(8,128)(2,1)S(1)} %copy.9.qr_hbm, bf16[8,128,512]{2,1,0:T(8,128)(2,1)S(1)} %copy-done, ...), custom_call_target="tpu_custom_call" | custom-call | flops 6000000000 | bytes 5000000 | tf_op jit(solution)/shard_map/pallas_call | solution.py:210
  38.5 0.8 %copy.11 = bf16[256,8,128]{2,1,0:T(8,128)(2,1)} copy(bf16[256,8,128]{2,1,0:T(8,128)(2,1)S(1)} %shard_map.73) | data formatting | bytes 1048576
Async XLA Ops:
  0.0 2.3 %copy-start.2 = (bf16[256,8,128]{2,1,0:T(8,128)(2,1)S(1)}, bf16[256,8,128]{2,1,0:T(8,128)(2,1)}, u32[]{:S(2)}) copy-start(bf16[256,8,128]{2,1,0:T(8,128)(2,1)} %qn_hbm.1) | copy-start | bytes 1572868
  0.9 1.4 %copy-start.3 = (bf16[256,512]{1,0:T(8,128)(2,1)S(1)}, bf16[256,512]{1,0:T(8,128)(2,1)}, u32[]{:S(2)}) copy-start(bf16[256,512]{1,0:T(8,128)(2,1)} %ckv_ref.1) | copy-start | bytes 786436
  0.9 1.4 %copy-start.4 = (s32[32]{0:T(128)S(1)}, s32[32]{0:T(128)}, u32[]{:S(2)}) copy-start(s32[32]{0:T(128)} %pos_ref.1) | copy-start | bytes 388
  2.3 1.2 %copy-start = (bf16[8,128,512]{2,1,0:T(8,128)(2,1)S(1)}, bf16[8,128,512]{2,1,0:T(8,128)(2,1)}, u32[]{:S(2)}) copy-start(bf16[8,128,512]{2,1,0:T(8,128)(2,1)} %wuk_hbm.1) | copy-start | bytes 3145732
  3.5 1.2 %copy-start.1 = (bf16[8,512,128]{2,1,0:T(8,128)(2,1)S(1)}, bf16[8,512,128]{2,1,0:T(8,128)(2,1)}, u32[]{:S(2)}) copy-start(bf16[8,512,128]{2,1,0:T(8,128)(2,1)} %wuv_hbm.1) | copy-start | bytes 3145732

commit v2 on v1

v2 whole, which is shorter than its diff:
```python
import functools
import math

import jax
import jax.numpy as jnp
from jax import lax
from jax.experimental import pallas as pl
from jax.experimental.pallas import tpu as pltpu
from jax.sharding import PartitionSpec as P

MESH = pl.DeviceIdType.MESH
LANES = 128
PIECES = ((0, 5), (5, 4))
PARTNER, NEAR, FAR, WIDE = 0, 1, 2, 3


def attention_kernel(
    factor,
    pos_ref, ckv_ref, krope_ref, qn_hbm, qr_hbm, wuk_hbm, wuv_hbm, out_ref,
    qn, qr, wuk, wuv, flat, qs, held, keys, values, acc, top_s, sum_s, wall,
    load_sem, send_sem, recv_sem,
):
    n = lax.axis_size("ctx")
    me = lax.axis_index("ctx")
    heads = qn.shape[1]
    blk = ckv_ref.shape[0] // 2
    lat = ckv_ref.shape[1]
    rope = krope_ref.shape[0]
    odd = lax.rem(me, 2)

    def at(by):
        return lax.rem(me + by + n, n)

    partner = at(1 - 2 * odd)
    near = at(2 * odd - 1)
    far = at(4 * odd - 2)
    wide = at(2 - 4 * odd)

    loads = [
        pltpu.make_async_copy(a, b, load_sem.at[i])
        for i, (a, b) in enumerate(
            ((qn_hbm, qn), (wuk_hbm, wuk), (qr_hbm, qr), (wuv_hbm, wuv))
        )
    ]
    for load in loads:
        load.start()

    barrier = pltpu.get_barrier_semaphore()
    for other in (partner, near, far, wide):
        pl.semaphore_signal(barrier, inc=1, device_id={"ctx": other}, device_id_type=MESH)

    for c in range(4):
        held[4, c] = ckv_ref[:blk, c * LANES:(c + 1) * LANES]
        held[4, 5 + c] = ckv_ref[blk:, c * LANES:(c + 1) * LANES]
    held[4, 4, :, :rope] = krope_ref[:, :blk].T
    held[4, 4, :, rope:] = krope_ref[:, blk:].T
    pl.semaphore_wait(barrier, 4)

    def send(slot_from, slot_to, piece, target):
        start, size = PIECES[piece]
        return pltpu.make_async_remote_copy(
            src_ref=held.at[slot_from, pl.ds(start, size)],
            dst_ref=held.at[slot_to, pl.ds(start, size)],
            send_sem=send_sem.at[slot_to, piece],
            recv_sem=recv_sem.at[slot_to, piece],
            device_id={"ctx": target},
            device_id_type=MESH,
        )

    copies = {}
    for piece in (0, 1):
        for slot, target in ((NEAR, near), (FAR, wide), (PARTNER, partner)):
            copies[slot, piece] = send(4, slot, piece, target)
            copies[slot, piece].start()
        copies[WIDE, piece] = send(NEAR, WIDE, piece, partner)

    loads[0].wait()
    flat[...] = qn[...].astype(jnp.float32).reshape(flat.shape)
    loads[1].wait()
    loads[2].wait()
    for h in range(heads):
        part = flat[pl.ds(h, 2 * blk, stride=heads), :].astype(jnp.bfloat16)
        turned = jnp.dot(part, wuk[h], preferred_element_type=jnp.float32).astype(jnp.bfloat16).T
        for b in range(2):
            into = pl.ds(h * blk, blk)
            qs[b, :lat, into] = turned[:, b * blk:(b + 1) * blk]
            rotary = qr[h, :, b * blk:(b + 1) * blk]
            qs[b, lat:lat + rope, into] = rotary
            qs[b, lat + rope:, into] = rotary

    my_pos = pos_ref[2 * me]
    lane = lax.broadcasted_iota(jnp.int32, (blk, LANES), 1)
    wall[...] = jnp.where(
        lax.broadcasted_iota(jnp.int32, (blk, blk), 0)
        <= lax.broadcasted_iota(jnp.int32, (blk, blk), 1),
        0.0,
        -1e30,
    )
    chunk = qs.shape[2] // 2

    def gather(slot, low_at, high_at):
        for base, first in ((low_at, 0), (high_at, 5)):
            for c in range(4):
                piece = held[slot, first + c]
                keys[pl.ds(base, blk), c * LANES:(c + 1) * LANES] = piece
                values[c * LANES:(c + 1) * LANES, pl.ds(base, blk)] = piece.T
        both = held[slot, 4]
        zero = jnp.zeros_like(both)
        keys[pl.ds(low_at, blk), lat:] = jnp.where(lane < rope, both, zero)
        keys[pl.ds(high_at, blk), lat:] = jnp.where(lane < rope, zero, both)

    def fold(b, columns, hides, first):
        width = len(hides) * blk
        score = jnp.dot(
            keys[:width, :], qs[b, :, columns], preferred_element_type=jnp.float32
        ) * factor
        parts = []
        for i, hide in enumerate(hides):
            part = score[i * blk:(i + 1) * blk]
            if hide is wall:
                part = part + jnp.concatenate([wall[...]] * (chunk // blk), axis=1)
            elif hide is not None:
                part = part + hide
            parts.append(part)
        best = functools.reduce(jnp.maximum, parts)
        best = jnp.max(best, axis=0, keepdims=True)
        if not first:
            old = top_s[b, :1, columns]
            best = jnp.maximum(best, old)
        parts = [jnp.exp2(part - best) for part in parts]
        total = jnp.sum(functools.reduce(jnp.add, parts), axis=0, keepdims=True)
        weights = jnp.concatenate([part.astype(jnp.bfloat16) for part in parts], axis=0)
        mixed = jnp.dot(values[:, :width], weights, preferred_element_type=jnp.float32)
        if not first:
            shrink = jnp.exp2(old - best)
            total = total + sum_s[b, :1, columns] * shrink
            mixed = mixed + acc[b, :, columns] * shrink
        acc[b, :, columns] = mixed
        top_s[b, :1, columns] = best
        sum_s[b, :1, columns] = total

    def stage(slots, sources, first):
        count = len(slots)
        low, high = [], []
        for i, (slot, source) in enumerate(zip(slots, sources)):
            gather(slot, i * blk, (count + i) * blk)
            if source is None:
                low.append(wall)
                high.append(wall)
            else:
                theirs = pos_ref[2 * source]
                low.append(jnp.where(theirs <= my_pos, 0.0, -1e30))
                high.append(jnp.where(theirs >= my_pos, 0.0, -1e30))

        def body(c, carry):
            columns = pl.ds(pl.multiple_of(c * chunk, chunk), chunk)
            fold(1, columns, [None] * count + high, first)
            fold(0, columns, low, first)
            return carry

        lax.fori_loop(0, 2, body, 0)

    loads[3].wait()
    copies[PARTNER, 0].wait_recv()
    copies[PARTNER, 1].wait_recv()
    stage((4, PARTNER), (None, partner), True)

    for piece in (0, 1):
        copies[NEAR, piece].wait_recv()
        copies[WIDE, piece].start()
    copies[FAR, 0].wait_recv()
    copies[FAR, 1].wait_recv()
    stage((NEAR, FAR), (near, far), False)
    copies[WIDE, 0].wait_recv()
    copies[WIDE, 1].wait_recv()
    stage((WIDE,), (wide,), False)

    for h in range(heads):
        for b in range(2):
            columns = pl.ds(h * blk, blk)
            o_lat = (acc[b, :, columns] / sum_s[b, :1, columns]).astype(jnp.bfloat16)
            flat[pl.ds(b * blk * heads + h, blk, stride=heads), :] = jnp.dot(
                o_lat.T, wuv[h], preferred_element_type=jnp.float32
            )
    out_ref[...] = flat[...].reshape(out_ref.shape).astype(jnp.bfloat16)
    for key in copies:
        copies[key].wait_send()


def per_device(q_nope, q_rope, c_kv, k_rope, block_pos, w_uk, w_uv):
    rows, heads, nope = q_nope.shape
    blk = rows // 2
    lat = c_kv.shape[1]
    rope = k_rope.shape[1]
    factor = math.log2(math.e) / math.sqrt(nope + rope)
    vmem = pl.BlockSpec(memory_space=pltpu.VMEM)
    anywhere = pl.BlockSpec(memory_space=pl.ANY)
    bf16, f32 = jnp.bfloat16, jnp.float32
    return pl.pallas_call(
        functools.partial(attention_kernel, factor),
        out_shape=jax.ShapeDtypeStruct((rows, heads, w_uv.shape[2]), bf16),
        in_specs=[pl.BlockSpec(memory_space=pltpu.SMEM), vmem, vmem] + [anywhere] * 4,
        out_specs=vmem,
        scratch_shapes=[
            pltpu.VMEM(q_nope.shape, bf16),
            pltpu.VMEM((heads, rope, rows), bf16),
            pltpu.VMEM(w_uk.shape, bf16),
            pltpu.VMEM(w_uv.shape, bf16),
            pltpu.VMEM((rows * heads, nope), f32),
            pltpu.VMEM((2, lat + 2 * rope, blk * heads), bf16),
            pltpu.VMEM((5, 9, blk, LANES), bf16),
            pltpu.VMEM((4 * blk, lat + 2 * rope), bf16),
            pltpu.VMEM((lat, 4 * blk), bf16),
            pltpu.VMEM((2, lat, blk * heads), f32),
            pltpu.VMEM((2, 8, blk * heads), f32),
            pltpu.VMEM((2, 8, blk * heads), f32),
            pltpu.VMEM((blk, blk), f32),
            pltpu.SemaphoreType.DMA((4,)),
            pltpu.SemaphoreType.DMA((4, 2)),
            pltpu.SemaphoreType.DMA((4, 2)),
        ],
        compiler_params=pltpu.CompilerParams(
            collective_id=0, has_side_effects=True, vmem_limit_bytes=60 * 1024 * 1024
        ),
        cost_estimate=pl.CostEstimate(
            flops=6 * 10**9, bytes_accessed=5 * 10**6, transcendentals=2 * 10**6
        ),
    )(block_pos, c_kv, k_rope.T, q_nope, jnp.transpose(q_rope, (1, 2, 0)), w_uk, w_uv)


def solution(mesh):
    placed = (
        P("ctx", "head", None),
        P("ctx", "head", None),
        P("ctx", None),
        P("ctx", None),
        P(),
        P("head", None, None),
        P("head", None, None),
    )
    return jax.shard_map(
        per_device, mesh=mesh, in_specs=placed, out_specs=P("ctx", "head", None), check_vma=False
    )
```

time: 39.5 us -> 28.5 us (0.72)
  Pallas kernels: 33.7 us -> 26.4 us
  local copies, waits for them, and re-layouts: 5.49 us -> 1.87 us
    pallas_call x1, Pallas kernels: 33.7 us -> 26.4 us  [per_device(): pl.pallas_call(functools.partial(attention_kernel, factor), out_shape=jax...]
    unnamed x13 -> x1, local copies, waits for them, and re-layouts: 5.49 us -> 1.87 us
where the time goes in v2:
time: 28.5 us; the launch traced here: 28.3 us
  Pallas kernels  26.4 us (93%)
  local copies, waits for them, and re-layouts  1.87 us (7%)
    pallas_call x1, Pallas kernels, per_device(): pl.pallas_call(functools.partial(attention_kernel, factor), out_shape=jax...  26.4 us
    unnamed x1, local copies, waits for them, and re-layouts  1.87 us

profile of v2, /device:TPU:1, one launch (start us, length us, event | category | flops | bytes accessed | tf_op | source)
XLA Modules:
  0.0 28.3 jit_solution(170245483492244348)
XLA Ops:
  0.0 26.4 %shard_map.73 = bf16[256,8,128]{2,1,0:T(8,128)(2,1)} custom-call(s32[32]{0:T(128)} %pos_ref.1, bf16[256,512]{1,0:T(8,128)(2,1)} %ckv_ref.1, bf16[64,256]{1,0:T(8,128)(2,1)} %bitcast.3, bf16[256,8,128]{2,1,0:T(8,128)(2,1)} %qn_hbm.1, bf16[8,64,256]{2,1,0:T(8,128)(2,1)} %bitcast.2, bf16[8,128,512]{2,1,0:T(8,128)(2,1)} %wuk_hbm.1, bf16[8,512,128]{2,1,0:T(8,128)(2,1)} %wuv_hbm.1), custom_call_target="tpu_custom_call" | custom-call | flops 6000000000 | bytes 5000000 | tf_op jit(solution)/shard_map/pallas_call | solution.py:199
  26.5 1.9 %copy.9 = bf16[256,8,128]{2,1,0:T(8,128)(2,1)} copy(bf16[256,8,128]{2,1,0:T(8,128)(2,1)} %shard_map.73) | data formatting | bytes 1048576

commit v3 on v2

--- a/solution.py
+++ b/solution.py
@@ -16,8 +16,8 @@
 
 def attention_kernel(
     factor,
-    pos_ref, ckv_ref, krope_ref, qn_hbm, qr_hbm, wuk_hbm, wuv_hbm, out_ref,
-    qn, qr, wuk, wuv, flat, qs, held, keys, values, acc, top_s, sum_s, wall,
+    pos_ref, ckv_hbm, krope_hbm, qn_hbm, qr_hbm, wuk_hbm, wuv_hbm, out_ref,
+    ckv_ref, krope_ref, qn, qr, wuk, wuv, flat, qs, held, keys, values, acc, top_s, sum_s, wall,
     load_sem, send_sem, recv_sem,
 ):
     n = lax.axis_size("ctx")
@@ -26,29 +26,37 @@
     blk = ckv_ref.shape[0] // 2
     lat = ckv_ref.shape[1]
     rope = krope_ref.shape[0]
-    odd = lax.rem(me, 2)
+    core = lax.rem(me, 2)
+    side = lax.rem(lax.div(me, 2), 2)
+    inner = lax.rem(core + side, 2)
+    toward = 1 - 2 * side
 
     def at(by):
         return lax.rem(me + by + n, n)
 
-    partner = at(1 - 2 * odd)
-    near = at(2 * odd - 1)
-    far = at(4 * odd - 2)
-    wide = at(2 - 4 * odd)
+    partner = at(1 - 2 * core)
+    near = at(2 * core - 1)
+    far = at(4 * core - 2)
+    wide = at(2 - 4 * core)
+    across = at(2 * toward)
+    relay = at(3 * toward * (2 * inner - 1))
 
     loads = [
         pltpu.make_async_copy(a, b, load_sem.at[i])
         for i, (a, b) in enumerate(
-            ((qn_hbm, qn), (wuk_hbm, wuk), (qr_hbm, qr), (wuv_hbm, wuv))
+            ((ckv_hbm, ckv_ref), (krope_hbm, krope_ref), (qn_hbm, qn),
+             (wuk_hbm, wuk), (qr_hbm, qr), (wuv_hbm, wuv))
         )
     ]
     for load in loads:
         load.start()
 
     barrier = pltpu.get_barrier_semaphore()
-    for other in (partner, near, far, wide):
+    for other in (partner, near, across, relay):
         pl.semaphore_signal(barrier, inc=1, device_id={"ctx": other}, device_id_type=MESH)
 
+    loads[0].wait()
+    loads[1].wait()
     for c in range(4):
         held[4, c] = ckv_ref[:blk, c * LANES:(c + 1) * LANES]
         held[4, 5 + c] = ckv_ref[blk:, c * LANES:(c + 1) * LANES]
@@ -56,28 +64,44 @@
     held[4, 4, :, rope:] = krope_ref[:, blk:].T
     pl.semaphore_wait(barrier, 4)
 
-    def send(slot_from, slot_to, piece, target):
+    def send(slot_from, slot_to, piece, target, flag=None):
         start, size = PIECES[piece]
         return pltpu.make_async_remote_copy(
             src_ref=held.at[slot_from, pl.ds(start, size)],
             dst_ref=held.at[slot_to, pl.ds(start, size)],
-            send_sem=send_sem.at[slot_to, piece],
+            send_sem=send_sem.at[slot_to if flag is None else flag, piece],
             recv_sem=recv_sem.at[slot_to, piece],
             device_id={"ctx": target},
             device_id_type=MESH,
         )
 
-    copies = {}
+    def arrived(slot, piece):
+        send(slot, slot, piece, partner).wait_recv()
+
+    own = []
     for piece in (0, 1):
-        for slot, target in ((NEAR, near), (FAR, wide), (PARTNER, partner)):
-            copies[slot, piece] = send(4, slot, piece, target)
-            copies[slot, piece].start()
-        copies[WIDE, piece] = send(NEAR, WIDE, piece, partner)
-
-    loads[0].wait()
+        own.append(send(4, 2 - inner, piece, at(toward * (2 - inner))))
+        own.append(send(4, PARTNER, piece, partner))
+    for copy in own:
+        copy.start()
+    forward = [send(NEAR, WIDE, piece, partner) for piece in (0, 1)]
+    relays = [
+        send(a, b, piece, relay, flag)
+        for piece in (0, 1)
+        for a, b, flag in ((FAR, NEAR, 4), (NEAR, FAR, FAR))
+    ]
+
+    def pass_on(piece):
+        arrived(FAR, piece)
+        relays[2 * piece].start()
+        arrived(NEAR, piece)
+        relays[2 * piece + 1].start()
+        forward[piece].start()
+
+    loads[2].wait()
     flat[...] = qn[...].astype(jnp.float32).reshape(flat.shape)
-    loads[1].wait()
-    loads[2].wait()
+    loads[3].wait()
+    loads[4].wait()
     for h in range(heads):
         part = flat[pl.ds(h, 2 * blk, stride=heads), :].astype(jnp.bfloat16)
         turned = jnp.dot(part, wuk[h], preferred_element_type=jnp.float32).astype(jnp.bfloat16).T
@@ -139,7 +163,7 @@
         top_s[b, :1, columns] = best
         sum_s[b, :1, columns] = total
 
-    def stage(slots, sources, first):
+    def stage(slots, sources, first, between=None):
         count = len(slots)
         low, high = [], []
         for i, (slot, source) in enumerate(zip(slots, sources)):
@@ -153,27 +177,45 @@
                 high.append(jnp.where(theirs >= my_pos, 0.0, -1e30))
 
         def body(c, carry):
-            columns = pl.ds(pl.multiple_of(c * chunk, chunk), chunk)
+            columns = pl.ds(c * chunk if isinstance(c, int) else pl.multiple_of(c * chunk, chunk), chunk)
             fold(1, columns, [None] * count + high, first)
             fold(0, columns, low, first)
             return carry
 
-        lax.fori_loop(0, 2, body, 0)
-
-    loads[3].wait()
-    copies[PARTNER, 0].wait_recv()
-    copies[PARTNER, 1].wait_recv()
-    stage((4, PARTNER), (None, partner), True)
-
-    for piece in (0, 1):
-        copies[NEAR, piece].wait_recv()
-        copies[WIDE, piece].start()
-    copies[FAR, 0].wait_recv()
-    copies[FAR, 1].wait_recv()
-    stage((NEAR, FAR), (near, far), False)
-    copies[WIDE, 0].wait_recv()
-    copies[WIDE, 1].wait_recv()
+        if between is None:
+            lax.fori_loop(0, 2, body, 0)
+        else:
+            body(0, 0)
+            between()
+            body(1, 0)
+
+    def pass_low():
+        @pl.when(inner == 1)
+        def _():
+            pass_on(0)
+
+    loads[5].wait()
+    arrived(PARTNER, 0)
+    arrived(PARTNER, 1)
+    stage((4, PARTNER), (None, partner), True, pass_low)
+
+    @pl.when(inner == 1)
+    def _():
+        pass_on(1)
+        stage((NEAR, FAR), (near, far), False)
+
+    arrived(WIDE, 0)
+    arrived(WIDE, 1)
     stage((WIDE,), (wide,), False)
+
+    @pl.when(inner == 0)
+    def _():
+        for piece in (0, 1):
+            arrived(NEAR, piece)
+            forward[piece].start()
+        arrived(FAR, 0)
+        arrived(FAR, 1)
+        stage((NEAR, FAR), (near, far), False)
 
     for h in range(heads):
         for b in range(2):
@@ -183,8 +225,13 @@
                 o_lat.T, wuv[h], preferred_element_type=jnp.float32
             )
     out_ref[...] = flat[...].reshape(out_ref.shape).astype(jnp.bfloat16)
-    for key in copies:
-        copies[key].wait_send()
+    for copy in own + forward:
+        copy.wait_send()
+
+    @pl.when(inner == 1)
+    def _():
+        for copy in relays:
+            copy.wait_send()
 
 
 def per_device(q_nope, q_rope, c_kv, k_rope, block_pos, w_uk, w_uv):
@@ -194,14 +241,16 @@
     rope = k_rope.shape[1]
     factor = math.log2(math.e) / math.sqrt(nope + rope)
     vmem = pl.BlockSpec(memory_space=pltpu.VMEM)
-    anywhere = pl.BlockSpec(memory_space=pl.ANY)
+    anywhere = pl.BlockSpec(memory_space=pltpu.HBM)
     bf16, f32 = jnp.bfloat16, jnp.float32
     return pl.pallas_call(
         functools.partial(attention_kernel, factor),
         out_shape=jax.ShapeDtypeStruct((rows, heads, w_uv.shape[2]), bf16),
-        in_specs=[pl.BlockSpec(memory_space=pltpu.SMEM), vmem, vmem] + [anywhere] * 4,
+        in_specs=[pl.BlockSpec(memory_space=pltpu.SMEM)] + [anywhere] * 6,
         out_specs=vmem,
         scratch_shapes=[
+            pltpu.VMEM(c_kv.shape, bf16),
+            pltpu.VMEM((rope, rows), bf16),
             pltpu.VMEM(q_nope.shape, bf16),
             pltpu.VMEM((heads, rope, rows), bf16),
             pltpu.VMEM(w_uk.shape, bf16),
@@ -215,12 +264,12 @@
             pltpu.VMEM((2, 8, blk * heads), f32),
             pltpu.VMEM((2, 8, blk * heads), f32),
             pltpu.VMEM((blk, blk), f32),
-            pltpu.SemaphoreType.DMA((4,)),
-            pltpu.SemaphoreType.DMA((4, 2)),
+            pltpu.SemaphoreType.DMA((6,)),
+            pltpu.SemaphoreType.DMA((5, 2)),
             pltpu.SemaphoreType.DMA((4, 2)),
         ],
         compiler_params=pltpu.CompilerParams(
-            collective_id=0, has_side_effects=True, vmem_limit_bytes=60 * 1024 * 1024
+            collective_id=0, has_side_effects=True, vmem_limit_bytes=40 * 1024 * 1024
         ),
         cost_estimate=pl.CostEstimate(
             flops=6 * 10**9, bytes_accessed=5 * 10**6, transcendentals=2 * 10**6

time: 28.5 us -> 31.3 us (1.098)
  the two profiles are of different devices: /device:TPU:1 before, /device:TPU:0 now
where the time goes in v3:
time: 31.3 us; the launch traced here: 30.9 us
  Pallas kernels  23.3 us (74%)
  local copies, waits for them, and re-layouts  7.6 us (24%)
    pallas_call x1, Pallas kernels, per_device(): pl.pallas_call(functools.partial(attention_kernel, factor), out_shape=jax...  23.3 us
    unnamed x15, local copies, waits for them, and re-layouts  7.6 us

profile of v3, /device:TPU:0, one launch (start us, length us, event | category | flops | bytes accessed | tf_op | source)
XLA Modules:
  0.0 30.9 jit_solution(2593016044272892619)
XLA Ops:
  0.0 0.0 copy-start.6
  0.0 0.7 %copy-done.6 = s32[32]{0:T(128)S(1)} copy-done((s32[32]{0:T(128)S(1)}, s32[32]{0:T(128)}, u32[]{:S(2)}) %copy-start.6) | copy-done | bytes 152
  0.7 0.0 copy-start
  0.7 1.2 %copy-done = bf16[8,128,512]{2,1,0:T(8,128)(2,1)S(1)} copy-done((bf16[8,128,512]{2,1,0:T(8,128)(2,1)S(1)}, bf16[8,128,512]{2,1,0:T(8,128)(2,1)}, u32[]{:S(2)}) %copy-start) | copy-done | bytes 1048600
  1.9 0.0 copy-start.1
  1.9 1.2 %copy-done.1 = bf16[8,512,128]{2,1,0:T(8,128)(2,1)S(1)} copy-done((bf16[8,512,128]{2,1,0:T(8,128)(2,1)S(1)}, bf16[8,512,128]{2,1,0:T(8,128)(2,1)}, u32[]{:S(2)}) %copy-start.1) | copy-done | bytes 1048600
  3.1 0.0 copy-start.2
  3.1 1.0 %copy-done.2 = bf16[256,8,128]{2,1,0:T(8,128)(2,1)S(1)} copy-done((bf16[256,8,128]{2,1,0:T(8,128)(2,1)S(1)}, bf16[256,8,128]{2,1,0:T(8,128)(2,1)}, u32[]{:S(2)}) %copy-start.2) | copy-done | bytes 524312
  4.1 0.0 copy-start.3
  4.2 0.9 %copy-done.3 = bf16[256,512]{1,0:T(8,128)(2,1)S(1)} copy-done((bf16[256,512]{1,0:T(8,128)(2,1)S(1)}, bf16[256,512]{1,0:T(8,128)(2,1)}, u32[]{:S(2)}) %copy-start.3) | copy-done | bytes 262168
  5.1 0.0 copy-start.4
  5.1 0.9 %copy-done.4 = bf16[256,8,64]{0,2,1:T(8,128)(2,1)S(1)} copy-done((bf16[256,8,64]{0,2,1:T(8,128)(2,1)S(1)}, bf16[256,8,64]{0,2,1:T(8,128)(2,1)}, u32[]{:S(2)}) %copy-start.4) | copy-done | bytes 262168
  6.0 0.0 copy-start.5
  6.1 0.8 %copy-done.5 = bf16[256,64]{0,1:T(8,128)(2,1)S(1)} copy-done((bf16[256,64]{0,1:T(8,128)(2,1)S(1)}, bf16[256,64]{0,1:T(8,128)(2,1)}, u32[]{:S(2)}) %copy-start.5) | copy-done | bytes 32792
  6.8 23.3 %shard_map.73 = bf16[256,8,128]{2,1,0:T(8,128)(2,1)S(1)} custom-call(s32[32]{0:T(128)S(1)} %copy-done.6, bf16[256,512]{1,0:T(8,128)(2,1)S(1)} %copy-done.3, bf16[64,256]{1,0:T(8,128)(2,1)S(1)} %bitcast.3, bf16[256,8,128]{2,1,0:T(8,128)(2,1)S(1)} %copy-done.2, bf16[8,64,256]{2,1,0:T(8,128)(2,1)S(1)} %bitcast.2, bf16[8,128,512]{2,1,0:T(8,128)(2,1)S(1)} %copy-done, ...), custom_call_target="tpu_custom_call" | custom-call | flops 6000000000 | bytes 5000000 | tf_op jit(solution)/shard_map/pallas_call | solution.py:246
  30.1 0.8 %copy.9 = bf16[256,8,128]{2,1,0:T(8,128)(2,1)} copy(bf16[256,8,128]{2,1,0:T(8,128)(2,1)S(1)} %shard_map.73) | data formatting | bytes 1048576
Async XLA Ops:
  0.0 0.7 %copy-start.6 = (s32[32]{0:T(128)S(1)}, s32[32]{0:T(128)}, u32[]{:S(2)}) copy-start(s32[32]{0:T(128)} %pos_ref.1) | copy-start | bytes 388
  0.7 1.2 %copy-start = (bf16[8,128,512]{2,1,0:T(8,128)(2,1)S(1)}, bf16[8,128,512]{2,1,0:T(8,128)(2,1)}, u32[]{:S(2)}) copy-start(bf16[8,128,512]{2,1,0:T(8,128)(2,1)} %wuk_hbm.1) | copy-start | bytes 3145732
  1.9 1.2 %copy-start.1 = (bf16[8,512,128]{2,1,0:T(8,128)(2,1)S(1)}, bf16[8,512,128]{2,1,0:T(8,128)(2,1)}, u32[]{:S(2)}) copy-start(bf16[8,512,128]{2,1,0:T(8,128)(2,1)} %wuv_hbm.1) | copy-start | bytes 3145732
  3.1 1.0 %copy-start.2 = (bf16[256,8,128]{2,1,0:T(8,128)(2,1)S(1)}, bf16[256,8,128]{2,1,0:T(8,128)(2,1)}, u32[]{:S(2)}) copy-start(bf16[256,8,128]{2,1,0:T(8,128)(2,1)} %qn_hbm.1) | copy-start | bytes 1572868
  4.1 0.9 %copy-start.3 = (bf16[256,512]{1,0:T(8,128)(2,1)S(1)}, bf16[256,512]{1,0:T(8,128)(2,1)}, u32[]{:S(2)}) copy-start(bf16[256,512]{1,0:T(8,128)(2,1)} %ckv_hbm.1) | copy-start | bytes 786436
  5.1 0.9 %copy-start.4 = (bf16[256,8,64]{0,2,1:T(8,128)(2,1)S(1)}, bf16[256,8,64]{0,2,1:T(8,128)(2,1)}, u32[]{:S(2)}) copy-start(bf16[256,8,64]{0,2,1:T(8,128)(2,1)} %param.8) | copy-start | bytes 786436
  6.0 0.8 %copy-start.5 = (bf16[256,64]{0,1:T(8,128)(2,1)S(1)}, bf16[256,64]{0,1:T(8,128)(2,1)}, u32[]{:S(2)}) copy-start(bf16[256,64]{0,1:T(8,128)(2,1)} %param.10) | copy-start | bytes 98308

commit v4 on v3

--- a/solution.py
+++ b/solution.py
@@ -10,7 +10,7 @@
 
 MESH = pl.DeviceIdType.MESH
 LANES = 128
-PIECES = ((0, 5), (5, 4))
+PIECES = ((0, 3), (3, 2), (5, 2), (7, 2))
 PARTNER, NEAR, FAR, WIDE = 0, 1, 2, 3
 
 
@@ -79,15 +79,15 @@
         send(slot, slot, piece, partner).wait_recv()
 
     own = []
-    for piece in (0, 1):
+    for piece in range(len(PIECES)):
         own.append(send(4, 2 - inner, piece, at(toward * (2 - inner))))
         own.append(send(4, PARTNER, piece, partner))
     for copy in own:
         copy.start()
-    forward = [send(NEAR, WIDE, piece, partner) for piece in (0, 1)]
+    forward = [send(NEAR, WIDE, piece, partner) for piece in range(len(PIECES))]
     relays = [
         send(a, b, piece, relay, flag)
-        for piece in (0, 1)
+        for piece in range(len(PIECES))
         for a, b, flag in ((FAR, NEAR, 4), (NEAR, FAR, FAR))
     ]
 
@@ -122,21 +122,26 @@
     )
     chunk = qs.shape[2] // 2
 
-    def gather(slot, low_at, high_at):
-        for base, first in ((low_at, 0), (high_at, 5)):
-            for c in range(4):
-                piece = held[slot, first + c]
-                keys[pl.ds(base, blk), c * LANES:(c + 1) * LANES] = piece
-                values[c * LANES:(c + 1) * LANES, pl.ds(base, blk)] = piece.T
+    def gather_low(slot, base):
+        for c in range(4):
+            piece = held[slot, c]
+            keys[pl.ds(base, blk), c * LANES:(c + 1) * LANES] = piece
+            values[c * LANES:(c + 1) * LANES, pl.ds(base, blk)] = piece.T
         both = held[slot, 4]
-        zero = jnp.zeros_like(both)
-        keys[pl.ds(low_at, blk), lat:] = jnp.where(lane < rope, both, zero)
-        keys[pl.ds(high_at, blk), lat:] = jnp.where(lane < rope, zero, both)
-
-    def fold(b, columns, hides, first):
-        width = len(hides) * blk
+        keys[pl.ds(base, blk), lat:] = jnp.where(lane < rope, both, jnp.zeros_like(both))
+
+    def gather_high(slot, base):
+        for c in range(4):
+            piece = held[slot, 5 + c]
+            keys[pl.ds(base, blk), c * LANES:(c + 1) * LANES] = piece
+            values[c * LANES:(c + 1) * LANES, pl.ds(base, blk)] = piece.T
+        both = held[slot, 4]
+        keys[pl.ds(base, blk), lat:] = jnp.where(lane < rope, jnp.zeros_like(both), both)
+
+    def fold(b, columns, base, hides, first=False):
+        rows = pl.ds(base, len(hides) * blk)
         score = jnp.dot(
-            keys[:width, :], qs[b, :, columns], preferred_element_type=jnp.float32
+            keys[rows, :], qs[b, :, columns], preferred_element_type=jnp.float32
         ) * factor
         parts = []
         for i, hide in enumerate(hides):
@@ -154,7 +159,7 @@
         parts = [jnp.exp2(part - best) for part in parts]
         total = jnp.sum(functools.reduce(jnp.add, parts), axis=0, keepdims=True)
         weights = jnp.concatenate([part.astype(jnp.bfloat16) for part in parts], axis=0)
-        mixed = jnp.dot(values[:, :width], weights, preferred_element_type=jnp.float32)
+        mixed = jnp.dot(values[:, rows], weights, preferred_element_type=jnp.float32)
         if not first:
             shrink = jnp.exp2(old - best)
             total = total + sum_s[b, :1, columns] * shrink
@@ -163,64 +168,113 @@
         top_s[b, :1, columns] = best
         sum_s[b, :1, columns] = total
 
-    def stage(slots, sources, first, between=None):
-        count = len(slots)
-        low, high = [], []
-        for i, (slot, source) in enumerate(zip(slots, sources)):
-            gather(slot, i * blk, (count + i) * blk)
-            if source is None:
-                low.append(wall)
-                high.append(wall)
-            else:
-                theirs = pos_ref[2 * source]
-                low.append(jnp.where(theirs <= my_pos, 0.0, -1e30))
-                high.append(jnp.where(theirs >= my_pos, 0.0, -1e30))
-
-        def body(c, carry):
-            columns = pl.ds(c * chunk if isinstance(c, int) else pl.multiple_of(c * chunk, chunk), chunk)
-            fold(1, columns, [None] * count + high, first)
-            fold(0, columns, low, first)
+    def part_of(c):
+        return pl.ds(c * chunk if isinstance(c, int) else pl.multiple_of(c * chunk, chunk), chunk)
+
+    def both_chunks(body):
+        def step(c, carry):
+            body(part_of(c))
             return carry
 
-        if between is None:
-            lax.fori_loop(0, 2, body, 0)
-        else:
-            body(0, 0)
-            between()
-            body(1, 0)
-
-    def pass_low():
+        lax.fori_loop(0, 2, step, 0)
+
+    def low_hide(source):
+        return jnp.where(pos_ref[2 * source] <= my_pos, 0.0, -1e30)
+
+    def high_hide(source):
+        return jnp.where(pos_ref[2 * source] >= my_pos, 0.0, -1e30)
+
+    def inner_passes(piece):
         @pl.when(inner == 1)
         def _():
-            pass_on(0)
+            pass_on(piece)
+
+    def outer_passes(piece):
+        @pl.when(inner == 0)
+        def _():
+            arrived(NEAR, piece)
+            forward[piece].start()
 
     loads[5].wait()
-    arrived(PARTNER, 0)
-    arrived(PARTNER, 1)
-    stage((4, PARTNER), (None, partner), True, pass_low)
+    inner_passes(0)
+    for piece in range(len(PIECES)):
+        arrived(PARTNER, piece)
+    gather_low(4, 0)
+    gather_low(PARTNER, blk)
+    gather_high(4, 2 * blk)
+    gather_high(PARTNER, 3 * blk)
+    lows, highs = [wall, low_hide(partner)], [wall, high_hide(partner)]
+    fold(1, part_of(0), 0, [None, None] + highs, True)
+    fold(0, part_of(0), 0, lows, True)
+    inner_passes(1)
+    fold(1, part_of(1), 0, [None, None] + highs, True)
+    inner_passes(2)
+    fold(0, part_of(1), 0, lows, True)
+    inner_passes(3)
+
+    near_lows, near_highs = [low_hide(near), low_hide(far)], [high_hide(near), high_hide(far)]
 
     @pl.when(inner == 1)
     def _():
-        pass_on(1)
-        stage((NEAR, FAR), (near, far), False)
-
+        gather_low(NEAR, 0)
+        gather_low(FAR, blk)
+        gather_high(NEAR, 2 * blk)
+        gather_high(FAR, 3 * blk)
+
+        @both_chunks
+        def _(columns):
+            fold(1, columns, 0, [None, None] + near_highs)
+            fold(0, columns, 0, near_lows)
+
+    outer_passes(0)
     arrived(WIDE, 0)
     arrived(WIDE, 1)
-    stage((WIDE,), (wide,), False)
+    gather_low(WIDE, 0)
+
+    @both_chunks
+    def _(columns):
+        fold(1, columns, 0, [None])
+        fold(0, columns, 0, [low_hide(wide)])
+
+    outer_passes(1)
+    arrived(WIDE, 2)
+    arrived(WIDE, 3)
+    gather_high(WIDE, blk)
+
+    @both_chunks
+    def _(columns):
+        fold(1, columns, blk, [high_hide(wide)])
 
     @pl.when(inner == 0)
     def _():
-        for piece in (0, 1):
-            arrived(NEAR, piece)
-            forward[piece].start()
         arrived(FAR, 0)
         arrived(FAR, 1)
-        stage((NEAR, FAR), (near, far), False)
+        gather_low(NEAR, 0)
+        gather_low(FAR, blk)
+
+        @both_chunks
+        def _(columns):
+            fold(1, columns, 0, [None, None])
+            fold(0, columns, 0, near_lows)
+
+    outer_passes(2)
+    outer_passes(3)
+
+    @pl.when(inner == 0)
+    def _():
+        arrived(FAR, 2)
+        arrived(FAR, 3)
+        gather_high(NEAR, 2 * blk)
+        gather_high(FAR, 3 * blk)
+
+        @both_chunks
+        def _(columns):
+            fold(1, columns, 2 * blk, near_highs)
 
     for h in range(heads):
         for b in range(2):
             columns = pl.ds(h * blk, blk)
-            o_lat = (acc[b, :, columns] / sum_s[b, :1, columns]).astype(jnp.bfloat16)
+            o_lat = (acc[b, :, columns] * (1.0 / sum_s[b, :1, columns])).astype(jnp.bfloat16)
             flat[pl.ds(b * blk * heads + h, blk, stride=heads), :] = jnp.dot(
                 o_lat.T, wuv[h], preferred_element_type=jnp.float32
             )
@@ -265,11 +319,11 @@
             pltpu.VMEM((2, 8, blk * heads), f32),
             pltpu.VMEM((blk, blk), f32),
             pltpu.SemaphoreType.DMA((6,)),
-            pltpu.SemaphoreType.DMA((5, 2)),
-            pltpu.SemaphoreType.DMA((4, 2)),
+            pltpu.SemaphoreType.DMA((5, len(PIECES))),
+            pltpu.SemaphoreType.DMA((4, len(PIECES))),
         ],
         compiler_params=pltpu.CompilerParams(
-            collective_id=0, has_side_effects=True, vmem_limit_bytes=40 * 1024 * 1024
+            collective_id=0, has_side_effects=True, vmem_limit_bytes=60 * 1024 * 1024
         ),
         cost_estimate=pl.CostEstimate(
             flops=6 * 10**9, bytes_accessed=5 * 10**6, transcendentals=2 * 10**6

time: 31.3 us -> 25.4 us (0.81)
  the two profiles are of different devices: /device:TPU:0 before, /device:TPU:1 now
where the time goes in v4:
time: 25.4 us; the launch traced here: 25.2 us
  Pallas kernels  23.4 us (92%)
  local copies, waits for them, and re-layouts  1.87 us (7%)
    pallas_call x1, Pallas kernels, per_device(): pl.pallas_call(functools.partial(attention_kernel, factor), out_shape=jax...  23.4 us
    unnamed x1, local copies, waits for them, and re-layouts  1.87 us

profile of v4, /device:TPU:1, one launch (start us, length us, event | category | flops | bytes accessed | tf_op | source)
XLA Modules:
  0.0 25.2 jit_solution(7665840746207179653)
XLA Ops:
  0.0 23.4 %shard_map.73 = bf16[256,8,128]{2,1,0:T(8,128)(2,1)} custom-call(s32[32]{0:T(128)} %pos_ref.1, bf16[256,512]{1,0:T(8,128)(2,1)} %ckv_hbm.1, bf16[64,256]{1,0:T(8,128)(2,1)} %bitcast.3, bf16[256,8,128]{2,1,0:T(8,128)(2,1)} %qn_hbm.1, bf16[8,64,256]{2,1,0:T(8,128)(2,1)} %bitcast.2, bf16[8,128,512]{2,1,0:T(8,128)(2,1)} %wuk_hbm.1, bf16[8,512,128]{2,1,0:T(8,128)(2,1)} %wuv_hbm.1), custom_call_target="tpu_custom_call" | custom-call | flops 6000000000 | bytes 5000000 | tf_op jit(solution)/shard_map/pallas_call | solution.py:300
  23.4 1.9 %copy.9 = bf16[256,8,128]{2,1,0:T(8,128)(2,1)} copy(bf16[256,8,128]{2,1,0:T(8,128)(2,1)} %shard_map.73) | data formatting | bytes 1048576

commit v5 on v4

v5 whole, which is shorter than its diff:
```python
import functools
import math

import jax
import jax.numpy as jnp
from jax import lax
from jax.experimental import pallas as pl
from jax.experimental.pallas import tpu as pltpu
from jax.sharding import PartitionSpec as P

MESH = pl.DeviceIdType.MESH
LANES = 128
PARTNER, NEAR, FAR, WIDE = 0, 1, 2, 3


def attention_kernel(
    factor,
    pos_ref, ckv_hbm, krope_hbm, qn_hbm, qr_hbm, wuk_hbm, wuv_hbm, out_ref,
    ckv_ref, krope_ref, qn, qr, wuk, wuv, flat, qs, held, keys, values, acc, top_s, sum_s, wall,
    load_sem, send_sem, recv_sem,
):
    n = lax.axis_size("ctx")
    me = lax.axis_index("ctx")
    heads = qn.shape[1]
    blk = ckv_ref.shape[0] // 2
    lat = ckv_ref.shape[1]
    rope = krope_ref.shape[0]
    mine = lax.axis_index("head")
    core = lax.rem(me, 2)
    side = lax.rem(lax.div(me, 2), 2)
    inner = lax.rem(core + side, 2)
    toward = 1 - 2 * side

    def at(by):
        return lax.rem(me + by + n, n)

    partner = at(1 - 2 * core)
    near = at(2 * core - 1)
    far = at(4 * core - 2)
    wide = at(2 - 4 * core)
    across = at(2 * toward)
    relay = at(3 * toward * (2 * inner - 1))

    loads = [
        pltpu.make_async_copy(a, b, load_sem.at[i])
        for i, (a, b) in enumerate(
            ((ckv_hbm, ckv_ref), (krope_hbm, krope_ref), (qn_hbm, qn),
             (wuk_hbm, wuk), (qr_hbm, qr), (wuv_hbm, wuv))
        )
    ]
    for load in loads:
        load.start()

    barrier = pltpu.get_barrier_semaphore()
    for other in (partner, near, across, relay):
        pl.semaphore_signal(barrier, inc=1, device_id={"ctx": other}, device_id_type=MESH)
    pl.semaphore_signal(barrier, inc=1, device_id={"head": 1 - mine}, device_id_type=MESH)

    loads[0].wait()
    loads[1].wait()
    half = blk // 2
    for b in range(2):
        for c in range(4):
            for r in range(2):
                held[4, b, 2 * c + r] = ckv_ref[
                    pl.ds(b * blk + r * half, half), c * LANES:(c + 1) * LANES
                ]
        turned = krope_ref[:, b * blk:(b + 1) * blk].T
        held[4, b, 8, :, :rope] = turned[:half]
        held[4, b, 8, :, rope:] = turned[half:]
    pl.semaphore_wait(barrier, 5)

    def send(slot_from, slot_to, part, target, flag):
        return pltpu.make_async_remote_copy(
            src_ref=held.at[slot_from, part],
            dst_ref=held.at[slot_to, part],
            send_sem=send_sem.at[flag],
            recv_sem=recv_sem.at[slot_to, part],
            device_id=target,
            device_id_type=MESH,
        )

    def arrived(slot, part):
        send(slot, slot, part, {"ctx": partner}, 0).wait_recv()

    own = [
        send(4, 2 - inner, mine, {"ctx": at(toward * (2 - inner))}, 0),
        send(4, PARTNER, 0, {"ctx": partner}, 1),
        send(4, PARTNER, 1, {"ctx": partner}, 2),
    ]
    for copy in own:
        copy.start()
    relays = [send(NEAR, FAR, mine, {"ctx": relay}, 3), send(FAR, NEAR, mine, {"ctx": relay}, 4)]
    mirrored = [send(slot, slot, mine, {"head": 1 - mine}, 4 + slot) for slot in (NEAR, FAR)]
    forward = [
        send(NEAR, WIDE, mine, {"ctx": partner}, 7),
        send(NEAR, WIDE, 1 - mine, {"ctx": partner}, 8),
    ]

    def pass_mine(relayed):
        for i, slot in enumerate((NEAR, FAR)):
            arrived(slot, mine)
            if relayed:
                relays[i].start()
            mirrored[i].start()
        forward[0].start()

    def pass_theirs():
        arrived(NEAR, 1 - mine)
        forward[1].start()
        arrived(FAR, 1 - mine)

    loads[2].wait()
    flat[...] = qn[...].astype(jnp.float32).reshape(flat.shape)
    loads[3].wait()
    loads[4].wait()
    for h in range(heads):
        part = flat[pl.ds(h, 2 * blk, stride=heads), :].astype(jnp.bfloat16)
        turned = jnp.dot(part, wuk[h], preferred_element_type=jnp.float32).astype(jnp.bfloat16).T
        for b in range(2):
            into = pl.ds(h * blk, blk)
            qs[b, :lat, into] = turned[:, b * blk:(b + 1) * blk]
            rotary = qr[h, :, b * blk:(b + 1) * blk]
            qs[b, lat:lat + rope, into] = rotary
            qs[b, lat + rope:, into] = rotary

    my_pos = pos_ref[2 * me]
    lane = lax.broadcasted_iota(jnp.int32, (half, LANES), 1)
    wall[...] = jnp.where(
        lax.broadcasted_iota(jnp.int32, (blk, blk), 0)
        <= lax.broadcasted_iota(jnp.int32, (blk, blk), 1),
        0.0,
        -1e30,
    )
    chunk = qs.shape[2] // 2

    def gather(slot, part, base):
        for c in range(4):
            tile = held[slot, part, 2 * c:2 * c + 2].reshape(blk, LANES)
            keys[pl.ds(base, blk), c * LANES:(c + 1) * LANES] = tile
            values[c * LANES:(c + 1) * LANES, pl.ds(base, blk)] = tile.T
        both = held[slot, part, 8]
        zero = jnp.zeros_like(both)
        keys[pl.ds(base, half), lat:] = jnp.where(lane < rope, both, zero)
        keys[pl.ds(base + half, half), lat:] = jnp.where(lane < rope, zero, both)

    def fold(b, columns, base, hides, first=False):
        rows = pl.ds(base, len(hides) * blk)
        score = jnp.dot(
            keys[rows, :], qs[b, :, columns], preferred_element_type=jnp.float32
        ) * factor
        parts = []
        for i, hide in enumerate(hides):
            part = score[i * blk:(i + 1) * blk]
            if hide is wall:
                part = part + jnp.concatenate([wall[...]] * (chunk // blk), axis=1)
            elif hide is not None:
                part = part + hide
            parts.append(part)
        best = functools.reduce(jnp.maximum, parts)
        best = jnp.max(best, axis=0, keepdims=True)
        if not first:
            old = top_s[b, :1, columns]
            best = jnp.maximum(best, old)
        parts = [jnp.exp2(part - best) for part in parts]
        total = jnp.sum(functools.reduce(jnp.add, parts), axis=0, keepdims=True)
        weights = jnp.concatenate([part.astype(jnp.bfloat16) for part in parts], axis=0)
        mixed = jnp.dot(values[:, rows], weights, preferred_element_type=jnp.float32)
        if not first:
            shrink = jnp.exp2(old - best)
            total = total + sum_s[b, :1, columns] * shrink
            mixed = mixed + acc[b, :, columns] * shrink
        acc[b, :, columns] = mixed
        top_s[b, :1, columns] = best
        sum_s[b, :1, columns] = total

    def part_of(c):
        return pl.ds(c * chunk if isinstance(c, int) else pl.multiple_of(c * chunk, chunk), chunk)

    def both_chunks(body):
        def step(c, carry):
            body(part_of(c))
            return carry

        lax.fori_loop(0, 2, step, 0)

    def low_hide(source):
        return jnp.where(pos_ref[2 * source] <= my_pos, 0.0, -1e30)

    def high_hide(source):
        return jnp.where(pos_ref[2 * source] >= my_pos, 0.0, -1e30)

    def when(cond):
        return lambda body: pl.when(cond)(body)

    loads[5].wait()
    arrived(PARTNER, 0)
    arrived(PARTNER, 1)
    for i, slot in enumerate((4, PARTNER)):
        gather(slot, 0, i * blk)
        gather(slot, 1, (2 + i) * blk)
    lows, highs = [wall, low_hide(partner)], [wall, high_hide(partner)]
    fold(1, part_of(0), 0, [None, None] + highs, True)

    @when(inner == 1)
    def _():
        pass_mine(True)

    fold(0, part_of(0), 0, lows, True)
    fold(1, part_of(1), 0, [None, None] + highs, True)
    fold(0, part_of(1), 0, lows, True)
    near_lows, near_highs = [low_hide(near), low_hide(far)], [high_hide(near), high_hide(far)]

    def low_unit():
        gather(NEAR, 0, 0)
        gather(FAR, 0, blk)

        @both_chunks
        def _(columns):
            fold(1, columns, 0, [None, None])
            fold(0, columns, 0, near_lows)

    def high_unit():
        gather(NEAR, 1, 2 * blk)
        gather(FAR, 1, 3 * blk)

        @both_chunks
        def _(columns):
            fold(1, columns, 2 * blk, near_highs)

    @when(inner == 1)
    def _():
        pass_theirs()
        for i, slot in enumerate((NEAR, FAR)):
            gather(slot, 0, i * blk)
            gather(slot, 1, (2 + i) * blk)

        @both_chunks
        def _(columns):
            fold(1, columns, 0, [None, None] + near_highs)
            fold(0, columns, 0, near_lows)

    @when(inner == 0)
    def _():
        pass_mine(False)

    arrived(WIDE, 0)
    arrived(WIDE, 1)
    gather(WIDE, 0, 0)
    gather(WIDE, 1, blk)

    @both_chunks
    def _(columns):
        fold(1, columns, 0, [None, high_hide(wide)])
        fold(0, columns, 0, [low_hide(wide)])

    @when(inner == 0)
    def _():
        when(mine == 0)(low_unit)
        when(mine == 1)(high_unit)
        pass_theirs()
        when(mine == 0)(high_unit)
        when(mine == 1)(low_unit)

    for h in range(heads):
        for b in range(2):
            columns = pl.ds(h * blk, blk)
            o_lat = (acc[b, :, columns] * (1.0 / sum_s[b, :1, columns])).astype(jnp.bfloat16)
            out_ref[h, pl.ds(b * blk, blk), :] = jnp.dot(
                o_lat.T, wuv[h], preferred_element_type=jnp.float32
            ).astype(jnp.bfloat16)
    for copy in own + mirrored + forward:
        copy.wait_send()

    @when(inner == 1)
    def _():
        for copy in relays:
            copy.wait_send()


def per_device(q_nope, q_rope, c_kv, k_rope, block_pos, w_uk, w_uv):
    rows, heads, nope = q_nope.shape
    blk = rows // 2
    lat = c_kv.shape[1]
    rope = k_rope.shape[1]
    factor = math.log2(math.e) / math.sqrt(nope + rope)
    vmem = pl.BlockSpec(memory_space=pltpu.VMEM)
    anywhere = pl.BlockSpec(memory_space=pltpu.HBM)
    bf16, f32 = jnp.bfloat16, jnp.float32
    out = pl.pallas_call(
        functools.partial(attention_kernel, factor),
        out_shape=jax.ShapeDtypeStruct((heads, rows, w_uv.shape[2]), bf16),
        in_specs=[pl.BlockSpec(memory_space=pltpu.SMEM)] + [anywhere] * 6,
        out_specs=vmem,
        scratch_shapes=[
            pltpu.VMEM(c_kv.shape, bf16),
            pltpu.VMEM((rope, rows), bf16),
            pltpu.VMEM(q_nope.shape, bf16),
            pltpu.VMEM((heads, rope, rows), bf16),
            pltpu.VMEM(w_uk.shape, bf16),
            pltpu.VMEM(w_uv.shape, bf16),
            pltpu.VMEM((rows * heads, nope), f32),
            pltpu.VMEM((2, lat + 2 * rope, blk * heads), bf16),
            pltpu.VMEM((5, 2, 9, blk // 2, LANES), bf16),
            pltpu.VMEM((4 * blk, lat + 2 * rope), bf16),
            pltpu.VMEM((lat, 4 * blk), bf16),
            pltpu.VMEM((2, lat, blk * heads), f32),
            pltpu.VMEM((2, 8, blk * heads), f32),
            pltpu.VMEM((2, 8, blk * heads), f32),
            pltpu.VMEM((blk, blk), f32),
            pltpu.SemaphoreType.DMA((6,)),
            pltpu.SemaphoreType.DMA((9,)),
            pltpu.SemaphoreType.DMA((4, 2)),
        ],
        compiler_params=pltpu.CompilerParams(
            collective_id=0, has_side_effects=True, vmem_limit_bytes=60 * 1024 * 1024
        ),
        cost_estimate=pl.CostEstimate(
            flops=6 * 10**9, bytes_accessed=5 * 10**6, transcendentals=2 * 10**6
        ),
    )(block_pos, c_kv, k_rope.T, q_nope, jnp.transpose(q_rope, (1, 2, 0)), w_uk, w_uv)
    return jnp.transpose(out, (1, 0, 2))


def solution(mesh):
    placed = (
        P("ctx", "head", None),
        P("ctx", "head", None),
        P("ctx", None),
        P("ctx", None),
        P(),
        P("head", None, None),
        P("head", None, None),
    )
    return jax.shard_map(
        per_device, mesh=mesh, in_specs=placed, out_specs=P("ctx", "head", None), check_vma=False
    )
```

time: 25.4 us -> 28.9 us (1.14)
  Pallas kernels: 23.4 us -> 26.6 us
  local copies, waits for them, and re-layouts: 1.87 us -> 2.18 us
    pallas_call x1, Pallas kernels: 23.4 us -> 26.6 us  [per_device(): pl.pallas_call(functools.partial(attention_kernel, factor), out_shape=jax...]
    transpose x0 -> x1, local copies, waits for them, and re-layouts: none -> 2.18 us  [per_device(): return jnp.transpose(out, (1, 0, 2))]
    unnamed x1 -> x0, local copies, waits for them, and re-layouts: 1.87 us -> none
where the time goes in v5:
time: 28.9 us; the launch traced here: 28.8 us
  Pallas kernels  26.6 us (92%)
  local copies, waits for them, and re-layouts  2.18 us (8%)
    pallas_call x1, Pallas kernels, per_device(): pl.pallas_call(functools.partial(attention_kernel, factor), out_shape=jax...  26.6 us
    transpose x1, local copies, waits for them, and re-layouts, per_device(): return jnp.transpose(out, (1, 0, 2))  2.18 us

profile of v5, /device:TPU:1, one launch (start us, length us, event | category | flops | bytes accessed | tf_op | source)
XLA Modules:
  0.0 28.8 jit_solution(3343946913239747064)
XLA Ops:
  0.0 26.6 %shard_map.73 = bf16[8,256,128]{2,1,0:T(8,128)(2,1)} custom-call(s32[32]{0:T(128)} %pos_ref.1, bf16[256,512]{1,0:T(8,128)(2,1)} %ckv_hbm.1, bf16[64,256]{1,0:T(8,128)(2,1)} %bitcast.5, bf16[256,8,128]{2,1,0:T(8,128)(2,1)} %qn_hbm.1, bf16[8,64,256]{2,1,0:T(8,128)(2,1)} %bitcast.4, bf16[8,128,512]{2,1,0:T(8,128)(2,1)} %wuk_hbm.1, bf16[8,512,128]{2,1,0:T(8,128)(2,1)} %wuv_hbm.1), custom_call_target="tpu_custom_call" | custom-call | flops 6000000000 | bytes 5000000 | tf_op jit(solution)/shard_map/pallas_call | solution.py:290
  26.6 2.2 %copy.8 = bf16[256,8,128]{2,1,0:T(8,128)(2,1)} copy(bf16[256,8,128]{2,0,1:T(8,128)(2,1)} %bitcast.3) | data formatting | bytes 1048576 | tf_op jit(solution)/shard_map/transpose | solution.py:322

commit v6 on v4

--- a/solution.py
+++ b/solution.py
@@ -104,7 +104,9 @@
     loads[4].wait()
     for h in range(heads):
         part = flat[pl.ds(h, 2 * blk, stride=heads), :].astype(jnp.bfloat16)
-        turned = jnp.dot(part, wuk[h], preferred_element_type=jnp.float32).astype(jnp.bfloat16).T
+        turned = lax.dot_general(
+            wuk[h], part, (((0,), (1,)), ((), ())), preferred_element_type=jnp.float32
+        ).astype(jnp.bfloat16)
         for b in range(2):
             into = pl.ds(h * blk, blk)
             qs[b, :lat, into] = turned[:, b * blk:(b + 1) * blk]
@@ -120,7 +122,7 @@
         0.0,
         -1e30,
     )
-    chunk = qs.shape[2] // 2
+    chunk = qs.shape[2] // 4
 
     def gather_low(slot, base):
         for c in range(4):
@@ -138,11 +140,15 @@
         both = held[slot, 4]
         keys[pl.ds(base, blk), lat:] = jnp.where(lane < rope, jnp.zeros_like(both), both)
 
-    def fold(b, columns, base, hides, first=False):
+    def score_of(task):
+        b, columns, base, hides, first = task
         rows = pl.ds(base, len(hides) * blk)
-        score = jnp.dot(
-            keys[rows, :], qs[b, :, columns], preferred_element_type=jnp.float32
-        ) * factor
+        return jnp.dot(keys[rows, :], qs[b, :, columns], preferred_element_type=jnp.float32)
+
+    def fold(task, score):
+        b, columns, base, hides, first = task
+        rows = pl.ds(base, len(hides) * blk)
+        score = score * factor
         parts = []
         for i, hide in enumerate(hides):
             part = score[i * blk:(i + 1) * blk]
@@ -168,12 +174,21 @@
         top_s[b, :1, columns] = best
         sum_s[b, :1, columns] = total
 
-    def part_of(c):
-        return pl.ds(c * chunk if isinstance(c, int) else pl.multiple_of(c * chunk, chunk), chunk)
-
-    def both_chunks(body):
+    def run(tasks):
+        ahead = score_of(tasks[0])
+        for i, task in enumerate(tasks):
+            score = ahead
+            if i + 1 < len(tasks):
+                ahead = score_of(tasks[i + 1])
+            fold(task, score)
+
+    def in_pairs(units):
         def step(c, carry):
-            body(part_of(c))
+            run([
+                (b, pl.ds(pl.multiple_of((2 * c + i) * chunk, chunk), chunk), base, hides, False)
+                for b, base, hides in units
+                for i in range(2)
+            ])
             return carry
 
         lax.fori_loop(0, 2, step, 0)
@@ -204,12 +219,10 @@
     gather_high(4, 2 * blk)
     gather_high(PARTNER, 3 * blk)
     lows, highs = [wall, low_hide(partner)], [wall, high_hide(partner)]
-    fold(1, part_of(0), 0, [None, None] + highs, True)
-    fold(0, part_of(0), 0, lows, True)
+    run([(1, pl.ds(c * chunk, chunk), 0, [None, None] + highs, True) for c in range(4)])
     inner_passes(1)
-    fold(1, part_of(1), 0, [None, None] + highs, True)
+    run([(0, pl.ds(c * chunk, chunk), 0, lows, True) for c in range(4)])
     inner_passes(2)
-    fold(0, part_of(1), 0, lows, True)
     inner_passes(3)
 
     near_lows, near_highs = [low_hide(near), low_hide(far)], [high_hide(near), high_hide(far)]
@@ -221,29 +234,21 @@
         gather_high(NEAR, 2 * blk)
         gather_high(FAR, 3 * blk)
 
-        @both_chunks
-        def _(columns):
-            fold(1, columns, 0, [None, None] + near_highs)
-            fold(0, columns, 0, near_lows)
+        in_pairs([(1, 0, [None, None] + near_highs), (0, 0, near_lows)])
 
     outer_passes(0)
     arrived(WIDE, 0)
     arrived(WIDE, 1)
     gather_low(WIDE, 0)
 
-    @both_chunks
-    def _(columns):
-        fold(1, columns, 0, [None])
-        fold(0, columns, 0, [low_hide(wide)])
+    in_pairs([(1, 0, [None]), (0, 0, [low_hide(wide)])])
 
     outer_passes(1)
     arrived(WIDE, 2)
     arrived(WIDE, 3)
     gather_high(WIDE, blk)
 
-    @both_chunks
-    def _(columns):
-        fold(1, columns, blk, [high_hide(wide)])
+    in_pairs([(1, blk, [high_hide(wide)])])
 
     @pl.when(inner == 0)
     def _():
@@ -252,10 +257,7 @@
         gather_low(NEAR, 0)
         gather_low(FAR, blk)
 
-        @both_chunks
-        def _(columns):
-            fold(1, columns, 0, [None, None])
-            fold(0, columns, 0, near_lows)
+        in_pairs([(1, 0, [None, None]), (0, 0, near_lows)])
 
     outer_passes(2)
     outer_passes(3)
@@ -267,9 +269,7 @@
         gather_high(NEAR, 2 * blk)
         gather_high(FAR, 3 * blk)
 
-        @both_chunks
-        def _(columns):
-            fold(1, columns, 2 * blk, near_highs)
+        in_pairs([(1, 2 * blk, near_highs)])
 
     for h in range(heads):
         for b in range(2):

time: 25.4 us -> 25.9 us (1.020)
  Pallas kernels: 23.4 us -> 23.8 us
    pallas_call x1, Pallas kernels: 23.4 us -> 23.8 us  [per_device(): pl.pallas_call(functools.partial(attention_kernel, factor), out_shape=jax...]
where the time goes in v6:
time: 25.9 us; the launch traced here: 25.7 us
  Pallas kernels  23.8 us (92%)
  local copies, waits for them, and re-layouts  1.87 us (7%)
    pallas_call x1, Pallas kernels, per_device(): pl.pallas_call(functools.partial(attention_kernel, factor), out_shape=jax...  23.8 us
    unnamed x1, local copies, waits for them, and re-layouts  1.87 us

profile of v6, /device:TPU:1, one launch (start us, length us, event | category | flops | bytes accessed | tf_op | source)
XLA Modules:
  0.0 25.7 jit_solution(4405420408264542498)
XLA Ops:
  0.0 23.8 %shard_map.73 = bf16[256,8,128]{2,1,0:T(8,128)(2,1)} custom-call(s32[32]{0:T(128)} %pos_ref.1, bf16[256,512]{1,0:T(8,128)(2,1)} %ckv_hbm.1, bf16[64,256]{1,0:T(8,128)(2,1)} %bitcast.3, bf16[256,8,128]{2,1,0:T(8,128)(2,1)} %qn_hbm.1, bf16[8,64,256]{2,1,0:T(8,128)(2,1)} %bitcast.2, bf16[8,128,512]{2,1,0:T(8,128)(2,1)} %wuk_hbm.1, bf16[8,512,128]{2,1,0:T(8,128)(2,1)} %wuv_hbm.1), custom_call_target="tpu_custom_call" | custom-call | flops 6000000000 | bytes 5000000 | tf_op jit(solution)/shard_map/pallas_call | solution.py:300
  23.9 1.9 %copy.9 = bf16[256,8,128]{2,1,0:T(8,128)(2,1)} copy(bf16[256,8,128]{2,1,0:T(8,128)(2,1)} %shard_map.73) | data formatting | bytes 1048576

commit v7 on v4

--- a/solution.py
+++ b/solution.py
@@ -104,7 +104,9 @@
     loads[4].wait()
     for h in range(heads):
         part = flat[pl.ds(h, 2 * blk, stride=heads), :].astype(jnp.bfloat16)
-        turned = jnp.dot(part, wuk[h], preferred_element_type=jnp.float32).astype(jnp.bfloat16).T
+        turned = lax.dot_general(
+            wuk[h], part, (((0,), (1,)), ((), ())), preferred_element_type=jnp.float32
+        ).astype(jnp.bfloat16)
         for b in range(2):
             into = pl.ds(h * blk, blk)
             qs[b, :lat, into] = turned[:, b * blk:(b + 1) * blk]
@@ -197,6 +199,7 @@
 
     loads[5].wait()
     inner_passes(0)
+    inner_passes(1)
     for piece in range(len(PIECES)):
         arrived(PARTNER, piece)
     gather_low(4, 0)
@@ -206,11 +209,10 @@
     lows, highs = [wall, low_hide(partner)], [wall, high_hide(partner)]
     fold(1, part_of(0), 0, [None, None] + highs, True)
     fold(0, part_of(0), 0, lows, True)
-    inner_passes(1)
+    inner_passes(2)
     fold(1, part_of(1), 0, [None, None] + highs, True)
-    inner_passes(2)
+    inner_passes(3)
     fold(0, part_of(1), 0, lows, True)
-    inner_passes(3)
 
     near_lows, near_highs = [low_hide(near), low_hide(far)], [high_hide(near), high_hide(far)]
 

time: 25.4 us -> 25.6 us (level)
  no operation moved by 1% of the time
where the time goes in v7:
time: 25.6 us; the launch traced here: 25.4 us
  Pallas kernels  23.5 us (92%)
  local copies, waits for them, and re-layouts  1.87 us (7%)
    pallas_call x1, Pallas kernels, per_device(): pl.pallas_call(functools.partial(attention_kernel, factor), out_shape=jax...  23.5 us
    unnamed x1, local copies, waits for them, and re-layouts  1.87 us

profile of v7, /device:TPU:1, one launch (start us, length us, event | category | flops | bytes accessed | tf_op | source)
XLA Modules:
  0.0 25.4 jit_solution(13424211558602177755)
XLA Ops:
  0.0 23.5 %shard_map.73 = bf16[256,8,128]{2,1,0:T(8,128)(2,1)} custom-call(s32[32]{0:T(128)} %pos_ref.1, bf16[256,512]{1,0:T(8,128)(2,1)} %ckv_hbm.1, bf16[64,256]{1,0:T(8,128)(2,1)} %bitcast.3, bf16[256,8,128]{2,1,0:T(8,128)(2,1)} %qn_hbm.1, bf16[8,64,256]{2,1,0:T(8,128)(2,1)} %bitcast.2, bf16[8,128,512]{2,1,0:T(8,128)(2,1)} %wuk_hbm.1, bf16[8,512,128]{2,1,0:T(8,128)(2,1)} %wuv_hbm.1), custom_call_target="tpu_custom_call" | custom-call | flops 6000000000 | bytes 5000000 | tf_op jit(solution)/shard_map/pallas_call | solution.py:302
  23.6 1.9 %copy.9 = bf16[256,8,128]{2,1,0:T(8,128)(2,1)} copy(bf16[256,8,128]{2,1,0:T(8,128)(2,1)} %shard_map.73) | data formatting | bytes 1048576

commit v8 on v4

--- a/solution.py
+++ b/solution.py
@@ -52,7 +52,7 @@
         load.start()
 
     barrier = pltpu.get_barrier_semaphore()
-    for other in (partner, near, across, relay):
+    for other in (partner, near, across, relay, at(4), at(-4)):
         pl.semaphore_signal(barrier, inc=1, device_id={"ctx": other}, device_id_type=MESH)
 
     loads[0].wait()
@@ -62,7 +62,7 @@
         held[4, 5 + c] = ckv_ref[blk:, c * LANES:(c + 1) * LANES]
     held[4, 4, :, :rope] = krope_ref[:, :blk].T
     held[4, 4, :, rope:] = krope_ref[:, blk:].T
-    pl.semaphore_wait(barrier, 4)
+    pl.semaphore_wait(barrier, 6)
 
     def send(slot_from, slot_to, piece, target, flag=None):
         start, size = PIECES[piece]
@@ -90,10 +90,12 @@
         for piece in range(len(PIECES))
         for a, b, flag in ((FAR, NEAR, 4), (NEAR, FAR, FAR))
     ]
+    onward = [send(FAR, WIDE, piece, at(4 * toward), 5) for piece in range(len(PIECES))]
 
     def pass_on(piece):
         arrived(FAR, piece)
         relays[2 * piece].start()
+        onward[piece].start()
         arrived(NEAR, piece)
         relays[2 * piece + 1].start()
         forward[piece].start()
@@ -193,7 +195,6 @@
         @pl.when(inner == 0)
         def _():
             arrived(NEAR, piece)
-            forward[piece].start()
 
     loads[5].wait()
     inner_passes(0)
@@ -279,12 +280,12 @@
                 o_lat.T, wuv[h], preferred_element_type=jnp.float32
             )
     out_ref[...] = flat[...].reshape(out_ref.shape).astype(jnp.bfloat16)
-    for copy in own + forward:
+    for copy in own:
         copy.wait_send()
 
     @pl.when(inner == 1)
     def _():
-        for copy in relays:
+        for copy in relays + forward + onward:
             copy.wait_send()
 
 
@@ -319,7 +320,7 @@
             pltpu.VMEM((2, 8, blk * heads), f32),
             pltpu.VMEM((blk, blk), f32),
             pltpu.SemaphoreType.DMA((6,)),
-            pltpu.SemaphoreType.DMA((5, len(PIECES))),
+            pltpu.SemaphoreType.DMA((6, len(PIECES))),
             pltpu.SemaphoreType.DMA((4, len(PIECES))),
         ],
         compiler_params=pltpu.CompilerParams(

time: 25.4 us -> 26.4 us (1.039)
  the two profiles are of different devices: /device:TPU:1 before, /device:TPU:0 now
where the time goes in v8:
time: 26.4 us; the launch traced here: 26.3 us
  Pallas kernels  24.4 us (92%)
  local copies, waits for them, and re-layouts  1.87 us (7%)
    pallas_call x1, Pallas kernels, per_device(): pl.pallas_call(functools.partial(attention_kernel, factor), out_shape=jax...  24.4 us
    unnamed x1, local copies, waits for them, and re-layouts  1.87 us

profile of v8, /device:TPU:0, one launch (start us, length us, event | category | flops | bytes accessed | tf_op | source)
XLA Modules:
  0.0 26.3 jit_solution(17722189355342068069)
XLA Ops:
  0.0 24.4 %shard_map.73 = bf16[256,8,128]{2,1,0:T(8,128)(2,1)} custom-call(s32[32]{0:T(128)} %pos_ref.1, bf16[256,512]{1,0:T(8,128)(2,1)} %ckv_hbm.1, bf16[64,256]{1,0:T(8,128)(2,1)} %bitcast.3, bf16[256,8,128]{2,1,0:T(8,128)(2,1)} %qn_hbm.1, bf16[8,64,256]{2,1,0:T(8,128)(2,1)} %bitcast.2, bf16[8,128,512]{2,1,0:T(8,128)(2,1)} %wuk_hbm.1, bf16[8,512,128]{2,1,0:T(8,128)(2,1)} %wuv_hbm.1), custom_call_target="tpu_custom_call" | custom-call | flops 6000000000 | bytes 5000000 | tf_op jit(solution)/shard_map/pallas_call | solution.py:301
  24.4 1.9 %copy.9 = bf16[256,8,128]{2,1,0:T(8,128)(2,1)} copy(bf16[256,8,128]{2,1,0:T(8,128)(2,1)} %shard_map.73) | data formatting | bytes 1048576
